TPU v7x, 512 devices: a whole 4x4x16 slice. The times are simulated.
512 devices in a mesh: mx: 32 (over y, x, core), my: 16 (over z).
Axes of the slice: x: 4, y: 4, z: 16, core: 2. Of those that a mesh axis runs over, the one named last changes fastest.
Arguments:
- block: float32 [32, 655360], P(None, ('mx', 'my')), may hold values from -6 to 6
- potential: float32 [655360], P(('mx', 'my')), may hold values from -1 to 1
- cell_nodes: int32 [125, 16384], P(None, ('mx', 'my')), may hold values from 0 to 2303
- cell_scale: float32 [16384], P(('mx', 'my')), may hold values from 0.5 to 2
- stiffness: float32 [125, 125], replicated, as said below
- send_nodes: int32 [8, 65536], P(None, ('mx', 'my')), may hold values from 0 to 1279
- proj_nodes: int32 [9, 1024, 256], P(None, ('mx', 'my')), may hold values from 0 to 1279
- proj_values: float32 [9, 1024, 18, 256], P(None, ('mx', 'my')), may hold values from -0.6 to 0.6
- coupling: float32 [1024, 18], P(('mx', 'my')), may hold values from -2 to 2
Outputs:
- filtered: float32 [32, 655360], P(None, ('mx', 'my'))
Inputs may be any that keep to these rules, and one draw needn't show every extreme that they name: `stiffness`: symmetric.
All inputs are finite; a program needn't handle non-finite values.
Results may differ from a plain program's by a relative error of at most 0.00015.
Values sent between devices are 32-bit elements; how exact they have to be, the bound alone decides.
A program may use at most 64 MiB of HBM per device.

v0:
```python
import jax
import jax.numpy as jnp
from jax import lax
from jax.sharding import PartitionSpec as P

DEGREES = 3


cheb_center = 5.0
cheb_half = 6.0


def passed_along(value, axis, steps):
    count = lax.axis_size(axis)
    pairs = [(source, (source + steps) % count) for source in range(count)]
    return lax.ppermute(value, axis, pairs)


def with_center(eight):
    zeros = jnp.zeros_like(eight[:1])
    joined = jnp.concatenate([eight[:4], zeros, eight[4:]], axis=0)
    return joined.reshape((3, 3) + eight.shape[1:])


def without_center(nine):
    flat = nine.reshape((9,) + nine.shape[2:])
    return jnp.concatenate([flat[:4], flat[5:]], axis=0)


def flipped(pack):
    return pack[::-1, ::-1]


def major_move(data, offset):
    return passed_along(data, "mx", offset)


def minor_move(data, offset):
    return passed_along(data, "my", offset)


def along_major(pack):
    return jnp.stack([major_move(pack[0], -1), pack[1], major_move(pack[2], 1)], axis=0)


def along_minor(pack):
    return jnp.stack([minor_move(pack[:, 0], -1), pack[:, 1], minor_move(pack[:, 2], 1)], axis=1)


def neighbours(pack):
    return along_minor(along_major(pack))


def shards(
    block,
    potential,
    cell_nodes,
    cell_scale,
    stiffness,
    send_nodes,
    proj_nodes,
    proj_values,
    coupling,
):
    vectors = block.shape[0]
    node_count = block.shape[1]
    send_count = send_nodes.shape[1]
    atom_count = coupling.shape[0]
    proj_count = coupling.shape[1]

    def apply(field):
        values = field[:, send_nodes].transpose(1, 0, 2)
        gathered = field[:, proj_nodes]
        partial_value = jnp.einsum(
            "kaps,vkas->kapv", proj_values, gathered, precision=lax.Precision.HIGHEST
        )
        partial_value = partial_value.reshape((3, 3, atom_count, proj_count, vectors))
        value_pack = with_center(values)
        ghost_pack = neighbours(value_pack)
        partial_in = neighbours(partial_value)
        scaled = coupling[:, :, None] * jnp.sum(partial_in, axis=(0, 1))
        spread = jnp.broadcast_to(scaled, (3, 3) + scaled.shape)
        coef = flipped(neighbours(spread))
        ghosts = without_center(ghost_pack).transpose(1, 0, 2).reshape(vectors, 8 * send_count)
        extended = jnp.concatenate([field, ghosts], axis=1)
        cellv = extended[:, cell_nodes]
        product = (
            jnp.einsum("pq,vqc->vpc", stiffness, cellv, precision=lax.Precision.HIGHEST)
            * cell_scale
        )
        assembled = jnp.zeros_like(extended).at[:, cell_nodes].add(product)
        own = assembled[:, :node_count]
        contrib = assembled[:, node_count:].reshape(vectors, 8, send_count).transpose(1, 0, 2)
        contrib_pack = flipped(with_center(contrib))
        back = flipped(neighbours(contrib_pack))
        own = own.at[:, send_nodes].add(without_center(back).transpose(1, 0, 2))
        added = jnp.einsum(
            "kaps,kapv->vkas",
            proj_values,
            coef.reshape(9, atom_count, proj_count, vectors),
            precision=lax.Precision.HIGHEST,
        )
        own = own.at[:, proj_nodes].add(added)
        return own + potential * field

    previous = block
    current = (apply(block) - cheb_center * block) / cheb_half
    for degree in range(DEGREES - 1):
        following = 2.0 * (apply(current) - cheb_center * current) / cheb_half - previous
        previous = current
        current = following
    return current


def solution(mesh):
    placed = (
        P(None, ("mx", "my")),
        P(("mx", "my")),
        P(None, ("mx", "my")),
        P(("mx", "my")),
        P(),
        P(None, ("mx", "my")),
        P(None, ("mx", "my"), None),
        P(None, ("mx", "my"), None, None),
        P(("mx", "my"), None),
    )
    return jax.shard_map(
        shards, mesh=mesh, in_specs=placed, out_specs=P(None, ("mx", "my")), check_vma=False
    )
```

profile of v0, /device:TPU:31, one launch (start us, length us, event | category | flops | bytes accessed | tf_op | source)
XLA Modules:
  0.0 535.4 jit_solution(11341136612325570922)
XLA Ops:
  1.9 2.8 gather_fusion
  5.5 2.6 collective-permute-start
  8.1 7.0 %collective-permute-start.1 = (f32[3,32,128]{2,1,0:T(8,128)}, f32[3,32,128]{2,1,0:T(8,128)}, u32[]{:S(2)}, u32[]{:S(2)}) collective-permute-start(f32[3,32,128]{2,1,0:T(8,128)} %get-tuple-element.83), channel_id=1, source_target_pairs={{0,16},{16,32},{32,48},{48,64},{64,80},{80,96},{96,112},{112,128},... | collective-permute-start | bytes 147464 | tf_op jit(solution)/shard_map/ppermute | solution.py:16
  15.2 7.3 %gather_fusion.2 = f32[4608,32]{1,0:T(8,128)S(1)} fusion(f32[32,1280]{0,1:T(8,128)S(1)} %copy.356, s32[5120]{0:T(1024)S(1)} %pad_clamp_fusion), kind=kCustom, calls=%fused_computation.2 | custom fusion | bytes 1198080 | tf_op jit(solution)/shard_map/gather | solution.py:73
  27.7 7.0 %collective-permute-start.9 = (f32[3,2,18,32]{3,2,1,0:T(8,128)S(1)}, f32[3,2,18,32]{3,2,1,0:T(8,128)S(1)}, u32[]{:S(2)}, u32[]{:S(2)}) collective-permute-start(f32[3,2,18,32]{3,2,1,0:T(8,128)S(1)} %get-tuple-element.30), channel_id=1, source_target_pairs={{0,16},{16,32},{32,48},{48,64},{64,80},{80,96},{96,112},{112,128},... | collective-permute-start | bytes 41480 | tf_op jit(solution)/shard_map/ppermute | solution.py:16
  36.1 2.8 collective-permute-start.11
  38.9 9.5 %collective-permute-start.10 = (f32[3,2,18,32]{3,2,1,0:T(8,128)S(1)}, f32[3,2,18,32]{3,2,1,0:T(8,128)S(1)}, u32[]{:S(2)}, u32[]{:S(2)}) collective-permute-start(f32[3,2,18,32]{3,2,1,0:T(8,128)S(1)} %get-tuple-element.28), channel_id=1, source_target_pairs={{0,15},{1,0},{2,1},{3,2},{4,3},{5,4},{6,5},{7,6},{8,7},{9,8},{10,9... | collective-permute-start | bytes 41480 | tf_op jit(solution)/shard_map/ppermute | solution.py:16
  49.9 8.4 %collective-permute-start.13 = (f32[3,2,18,32]{3,2,1,0:T(8,128)S(1)}, f32[3,2,18,32]{3,2,1,0:T(8,128)S(1)}, u32[]{:S(2)}, u32[]{:S(2)}) collective-permute-start(f32[3,2,18,32]{3,2,1,0:T(8,128)S(1)} %squeeze.122), channel_id=1, source_target_pairs={{0,16},{16,32},{32,48},{48,64},{64,80},{80,96},{96,112},{112,128},... | collective-permute-start | bytes 41480 | tf_op jit(solution)/shard_map/ppermute | solution.py:16
  60.3 7.0 %collective-permute-done.12 = f32[3,2,18,32]{3,2,1,0:T(8,128)S(1)} collective-permute-done((f32[3,2,18,32]{3,2,1,0:T(8,128)S(1)}, f32[3,2,18,32]{3,2,1,0:T(8,128)S(1)}, u32[]{:S(2)}, u32[]{:S(2)}) %collective-permute-start.12) | collective-permute-done | bytes 13856 | tf_op jit(solution)/shard_map/ppermute | solution.py:16
  67.4 5.2 collective-permute-start.14
  75.5 4.6 collective-permute-start.2
  86.6 14.2 %gather_fusion.1 = f32[4000,32]{1,0:T(8,128)} fusion(f32[32,2304]{0,1:T(8,128)S(1)} %copy.363, s32[4096]{0:T(1024)S(1)} %pad_clamp_fusion.1), kind=kCustom, calls=%fused_computation.1 | custom fusion | bytes 1040000 | tf_op jit(solution)/shard_map/gather | solution.py:86
  100.7 2.9 copy.364
  104.2 2.9 copy.433
  107.1 23.0 %scatter_custom_fusion = f32[32,2304]{0,1:T(8,128)S(1)} fusion(s32[4000]{0:T(1024)S(1)} %reshape.254, f32[4000,32]{1,0:T(8,128)} %bitcast.288, f32[]{:T(128)} %constant.8.clone.1), kind=kCustom, calls=%fused_computation.45 | custom fusion | flops 128000 | bytes 295424 | tf_op jit(solution)/shard_map/scatter-add | solution.py:91
  130.4 3.8 collective-permute-start.5
  136.3 6.7 %collective-permute-done.4 = f32[3,32,128]{2,1,0:T(8,128)S(1)} collective-permute-done((f32[3,32,128]{2,1,0:T(8,128)S(1)}, f32[3,32,128]{2,1,0:T(8,128)S(1)}, u32[]{:S(2)}, u32[]{:S(2)}) %collective-permute-start.4) | collective-permute-done | bytes 49184 | tf_op jit(solution)/shard_map/ppermute | solution.py:16
  143.0 2.5 collective-permute-start.6
  145.6 2.8 collective-permute-start.7
  148.6 3.0 collective-permute-done.7
  151.9 18.7 %scatter_fusion = f32[32,1280]{0,1:T(8,128)S(1)} fusion(f32[32,1280]{0,1:T(8,128)S(1)} %slice_add_fusion.2, s32[1024]{0:T(1024)S(1)} %fusion.27, f32[1024,32]{1,0:T(8,128)S(1)} %bitcast.307), kind=kCustom, calls=%fused_computation.10 | custom fusion | flops 32768 | bytes 397312 | tf_op jit(solution)/shard_map/scatter-add | solution.py:96
  170.6 25.6 %scatter_fusion.1 = f32[32,1280]{0,1:T(8,128)S(1)} fusion(f32[32,1280]{0,1:T(8,128)S(1)} %scatter_fusion, s32[4608]{0:T(1024)S(1)} %reshape.222, f32[4608,32]{1,0:T(8,128)} %bitcast.278), kind=kCustom, calls=%fused_computation.11 | custom fusion | flops 147456 | bytes 1787904 | tf_op jit(solution)/shard_map/scatter-add | solution.py:103
  196.4 2.8 gather_fusion.3
  199.2 9.3 %gather_fusion.5 = f32[4608,32]{1,0:T(8,128)} fusion(f32[32,1280]{0,1:T(8,128)S(1)} %broadcast_multiply_fusion, s32[5120]{0:T(1024)S(1)} %pad_clamp_fusion), kind=kCustom, calls=%fused_computation.5 | custom fusion | bytes 1198080 | tf_op jit(solution)/shard_map/gather | solution.py:73
  208.7 2.3 copy.400
  213.6 7.0 %collective-permute-start.25 = (f32[3,2,18,32]{3,2,1,0:T(8,128)S(1)}, f32[3,2,18,32]{3,2,1,0:T(8,128)S(1)}, u32[]{:S(2)}, u32[]{:S(2)}) collective-permute-start(f32[3,2,18,32]{3,2,1,0:T(8,128)S(1)} %get-tuple-element.21), channel_id=1, source_target_pairs={{0,16},{16,32},{32,48},{48,64},{64,80},{80,96},{96,112},{112,128},... | collective-permute-start | bytes 41480 | tf_op jit(solution)/shard_map/ppermute | solution.py:16
  223.9 4.6 collective-permute-start.26
  231.1 8.2 %collective-permute-start.17 = (f32[3,32,128]{2,1,0:T(8,128)}, f32[3,32,128]{2,1,0:T(8,128)S(1)}, u32[]{:S(2)}, u32[]{:S(2)}) collective-permute-start(f32[3,32,128]{2,1,0:T(8,128)} %get-tuple-element.75), channel_id=1, source_target_pairs={{0,16},{16,32},{32,48},{48,64},{64,80},{80,96},{96,112},{112,128},... | collective-permute-start | bytes 147464 | tf_op jit(solution)/shard_map/ppermute | solution.py:16
  239.4 2.4 collective-permute-start.29
  243.8 7.0 %collective-permute-done.28 = f32[3,2,18,32]{3,2,1,0:T(8,128)S(1)} collective-permute-done((f32[3,2,18,32]{3,2,1,0:T(8,128)S(1)}, f32[3,2,18,32]{3,2,1,0:T(8,128)S(1)}, u32[]{:S(2)}, u32[]{:S(2)}) %collective-permute-start.28) | collective-permute-done | bytes 13856 | tf_op jit(solution)/shard_map/ppermute | solution.py:16
  253.0 3.1 collective-permute-start.31
  256.8 3.4 collective-permute-start.18
  269.6 14.2 %gather_fusion.4 = f32[4000,32]{1,0:T(8,128)} fusion(f32[32,2304]{0,1:T(8,128)S(1)} %pad_maximum_fusion, s32[4096]{0:T(1024)S(1)} %pad_clamp_fusion.1), kind=kCustom, calls=%fused_computation.4 | custom fusion | bytes 1040000 | tf_op jit(solution)/shard_map/gather | solution.py:86
  283.8 2.9 copy.390
  287.2 2.9 copy.437
  290.1 23.0 %scatter_custom_fusion.3 = f32[32,2304]{0,1:T(8,128)S(1)} fusion(s32[4000]{0:T(1024)} %copy-done.9, f32[4000,32]{1,0:T(8,128)} %bitcast.289, f32[]{:T(128)} %constant.8.clone.1), kind=kCustom, calls=%fused_computation.43 | custom fusion | flops 128000 | bytes 295424 | tf_op jit(solution)/shard_map/scatter-add | solution.py:91
  313.4 3.8 collective-permute-start.21
  319.3 6.7 %collective-permute-done.20 = f32[3,32,128]{2,1,0:T(8,128)S(1)} collective-permute-done((f32[3,32,128]{2,1,0:T(8,128)S(1)}, f32[3,32,128]{2,1,0:T(8,128)S(1)}, u32[]{:S(2)}, u32[]{:S(2)}) %collective-permute-start.20) | collective-permute-done | bytes 49184 | tf_op jit(solution)/shard_map/ppermute | solution.py:16
  326.0 2.2 collective-permute-start.22
  328.2 3.1 collective-permute-start.23
  334.6 6.3 %scatter_fusion.2 = f32[32,1280]{0,1:T(8,128)S(1)} fusion(f32[32,1280]{0,1:T(8,128)S(1)} %slice_add_fusion.1, s32[1024]{0:T(1024)S(1)} %fusion.27, f32[1024,32]{1,0:T(8,128)S(1)} %bitcast.308), kind=kCustom, calls=%fused_computation.13 | custom fusion | flops 32768 | bytes 397312 | tf_op jit(solution)/shard_map/scatter-add | solution.py:96
  340.9 25.8 %scatter_fusion.3 = f32[32,1280]{0,1:T(8,128)S(1)} fusion(f32[32,1280]{0,1:T(8,128)S(1)} %scatter_fusion.2, s32[4608]{0:T(1024)S(1)} %reshape.222, f32[4608,32]{1,0:T(8,128)} %bitcast.277), kind=kCustom, calls=%fused_computation.14 | custom fusion | flops 147456 | bytes 1787904 | tf_op jit(solution)/shard_map/scatter-add | solution.py:103
  366.8 2.8 gather_fusion.6
  369.6 9.3 %gather_fusion.8 = f32[4608,32]{1,0:T(8,128)} fusion(f32[32,1280]{0,1:T(8,128)S(1)} %multiply_subtract_fusion.1, s32[5120]{0:T(1024)S(1)} %pad_clamp_fusion), kind=kCustom, calls=%fused_computation.8 | custom fusion | bytes 1198080 | tf_op jit(solution)/shard_map/gather | solution.py:73
  379.1 2.3 copy.424
  384.1 7.0 %collective-permute-start.41 = (f32[3,2,18,32]{3,2,1,0:T(8,128)S(1)}, f32[3,2,18,32]{3,2,1,0:T(8,128)S(1)}, u32[]{:S(2)}, u32[]{:S(2)}) collective-permute-start(f32[3,2,18,32]{3,2,1,0:T(8,128)S(1)} %get-tuple-element.12), channel_id=1, source_target_pairs={{0,16},{16,32},{32,48},{48,64},{64,80},{80,96},{96,112},{112,128},... | collective-permute-start | bytes 41480 | tf_op jit(solution)/shard_map/ppermute | solution.py:16
  394.4 4.6 collective-permute-start.42
  400.9 8.2 %collective-permute-start.33 = (f32[3,32,128]{2,1,0:T(8,128)S(1)}, f32[3,32,128]{2,1,0:T(8,128)S(1)}, u32[]{:S(2)}, u32[]{:S(2)}) collective-permute-start(f32[3,32,128]{2,1,0:T(8,128)S(1)} %get-tuple-element.67), channel_id=1, source_target_pairs={{0,16},{16,32},{32,48},{48,64},{64,80},{80,96},{96,112},{112,128},... | collective-permute-start | bytes 147464 | tf_op jit(solution)/shard_map/ppermute | solution.py:16
  409.3 2.4 collective-permute-start.45
  413.7 7.0 %collective-permute-done.44 = f32[3,2,18,32]{3,2,1,0:T(8,128)S(1)} collective-permute-done((f32[3,2,18,32]{3,2,1,0:T(8,128)S(1)}, f32[3,2,18,32]{3,2,1,0:T(8,128)S(1)}, u32[]{:S(2)}, u32[]{:S(2)}) %collective-permute-start.44) | collective-permute-done | bytes 13856 | tf_op jit(solution)/shard_map/ppermute | solution.py:16
  420.7 2.8 collective-permute-start.46
  423.5 2.5 collective-permute-start.47
  426.1 4.0 collective-permute-start.34
  436.5 14.2 %gather_fusion.7 = f32[4000,32]{1,0:T(8,128)} fusion(f32[32,2304]{0,1:T(8,128)S(1)} %pad_maximum_fusion.1, s32[4096]{0:T(1024)S(1)} %pad_clamp_fusion.1), kind=kCustom, calls=%fused_computation.7 | custom fusion | bytes 1040000 | tf_op jit(solution)/shard_map/gather | solution.py:86
  450.6 2.9 copy.414
  454.1 2.9 copy.441
  457.0 23.0 %scatter_custom_fusion.6 = f32[32,2304]{0,1:T(8,128)S(1)} fusion(s32[4000]{0:T(1024)} %copy-done.9, f32[4000,32]{1,0:T(8,128)} %bitcast.287, f32[]{:T(128)} %constant.8.clone.1), kind=kCustom, calls=%fused_computation.41 | custom fusion | flops 128000 | bytes 295424 | tf_op jit(solution)/shard_map/scatter-add | solution.py:91
  480.3 3.9 collective-permute-start.37
  486.2 6.7 %collective-permute-done.36 = f32[3,32,128]{2,1,0:T(8,128)S(1)} collective-permute-done((f32[3,32,128]{2,1,0:T(8,128)S(1)}, f32[3,32,128]{2,1,0:T(8,128)S(1)}, u32[]{:S(2)}, u32[]{:S(2)}) %collective-permute-start.36) | collective-permute-done | bytes 49184 | tf_op jit(solution)/shard_map/ppermute | solution.py:16
  492.9 2.5 collective-permute-start.38
  495.4 2.8 collective-permute-start.39
  498.5 3.0 collective-permute-done.39
  501.8 6.5 %scatter_fusion.4 = f32[32,1280]{0,1:T(8,128)S(1)} fusion(f32[32,1280]{0,1:T(8,128)S(1)} %slice_add_fusion, s32[1024]{0:T(1024)S(1)} %fusion.27, f32[1024,32]{1,0:T(8,128)S(1)} %bitcast.306), kind=kCustom, calls=%fused_computation.16 | custom fusion | flops 32768 | bytes 397312 | tf_op jit(solution)/shard_map/scatter-add | solution.py:96
  508.3 25.7 %scatter_fusion.5 = f32[32,1280]{0,1:T(8,128)S(1)} fusion(f32[32,1280]{0,1:T(8,128)S(1)} %scatter_fusion.4, s32[4608]{0:T(1024)S(1)} %reshape.222, f32[4608,32]{1,0:T(8,128)} %bitcast.276), kind=kCustom, calls=%fused_computation.17 | custom fusion | flops 147456 | bytes 1787904 | tf_op jit(solution)/shard_map/scatter-add | solution.py:103
  (243 shorter events, 75.4 us)
Async XLA Ops:
  0.0 24.0 %copy-start = (f32[9,2,18,256]{3,1,2,0:T(2,128)S(1)}, f32[9,2,18,256]{3,1,2,0:T(2,128)}, u32[]{:S(2)}) copy-start(f32[9,2,18,256]{3,1,2,0:T(2,128)} %param.16) | copy-start | bytes 995332
  0.0 15.2 %copy-start.10 = (s32[9,2,256]{2,1,0:T(2,128)S(1)}, s32[9,2,256]{2,1,0:T(2,128)}, u32[]{:S(2)}) copy-start(s32[9,2,256]{2,1,0:T(2,128)} %param.15) | copy-start | bytes 55300
  5.5 69.0 %collective-permute-start = (f32[3,32,128]{2,1,0:T(8,128)}, f32[3,32,128]{2,1,0:T(8,128)}, u32[]{:S(2)}, u32[]{:S(2)}) collective-permute-start(f32[3,32,128]{2,1,0:T(8,128)} %get-tuple-element.82), channel_id=1, source_target_pairs={{0,496},{16,0},{32,16},{48,32},{64,48},{80,64},{96,80},{112,96},{1... | collective-permute-start | bytes 147464 | tf_op jit(solution)/shard_map/ppermute | solution.py:16
  8.1 66.5 %collective-permute-start.1 = (f32[3,32,128]{2,1,0:T(8,128)}, f32[3,32,128]{2,1,0:T(8,128)}, u32[]{:S(2)}, u32[]{:S(2)}) collective-permute-start(f32[3,32,128]{2,1,0:T(8,128)} %get-tuple-element.83), channel_id=1, source_target_pairs={{0,16},{16,32},{32,48},{48,64},{64,80},{80,96},{96,112},{112,128},... | collective-permute-start | bytes 147464 | tf_op jit(solution)/shard_map/ppermute | solution.py:16
  22.5 12.3 %copy-start.11 = (s32[125,32]{0,1:T(8,128)S(1)}, s32[125,32]{0,1:T(8,128)}, u32[]{:S(2)}) copy-start(s32[125,32]{0,1:T(8,128)} %param.11) | copy-start | bytes 48004
  22.5 12.4 %copy-start.8 = (f32[1280]{0:T(1024)S(1)}, f32[1280]{0:T(1024)}, u32[]{:S(2)}) copy-start(f32[1280]{0:T(1024)} %param.10) | copy-start | bytes 15364
  24.0 24.4 %copy-start.12 = (s32[8,128]{1,0:T(8,128)S(1)}, s32[8,128]{1,0:T(8,128)}, u32[]{:S(2)}) copy-start(s32[8,128]{1,0:T(8,128)} %param.14) | copy-start | bytes 12292
  24.0 25.8 %copy-start.13 = (f32[2,18]{1,0:T(2,128)S(1)}, f32[2,18]{1,0:T(2,128)}, u32[]{:S(2)}) copy-start(f32[2,18]{1,0:T(2,128)} %param.17) | copy-start | bytes 436
  25.8 9.8 %collective-permute-start.8 = (f32[3,2,18,32]{3,2,1,0:T(8,128)S(1)}, f32[3,2,18,32]{3,2,1,0:T(8,128)S(1)}, u32[]{:S(2)}, u32[]{:S(2)}) collective-permute-start(f32[3,2,18,32]{3,2,1,0:T(8,128)S(1)} %get-tuple-element.29), channel_id=1, source_target_pairs={{0,496},{16,0},{32,16},{48,32},{64,48},{80,64},{96,80},{112,96},{1... | collective-permute-start | bytes 41480 | tf_op jit(solution)/shard_map/ppermute | solution.py:16
  27.7 8.4 %collective-permute-start.9 = (f32[3,2,18,32]{3,2,1,0:T(8,128)S(1)}, f32[3,2,18,32]{3,2,1,0:T(8,128)S(1)}, u32[]{:S(2)}, u32[]{:S(2)}) collective-permute-start(f32[3,2,18,32]{3,2,1,0:T(8,128)S(1)} %get-tuple-element.30), channel_id=1, source_target_pairs={{0,16},{16,32},{32,48},{48,64},{64,80},{80,96},{96,112},{112,128},... | collective-permute-start | bytes 41480 | tf_op jit(solution)/shard_map/ppermute | solution.py:16
  36.1 12.5 %collective-permute-start.11 = (f32[3,2,18,32]{3,2,1,0:T(8,128)S(1)}, f32[3,2,18,32]{3,2,1,0:T(8,128)S(1)}, u32[]{:S(2)}, u32[]{:S(2)}) collective-permute-start(f32[3,2,18,32]{3,2,1,0:T(8,128)S(1)} %get-tuple-element.27), channel_id=1, source_target_pairs={{0,1},{1,2},{2,3},{3,4},{4,5},{5,6},{6,7},{7,8},{8,9},{9,10},{10,1... | collective-permute-start | bytes 41480 | tf_op jit(solution)/shard_map/ppermute | solution.py:16
  38.9 10.9 %collective-permute-start.10 = (f32[3,2,18,32]{3,2,1,0:T(8,128)S(1)}, f32[3,2,18,32]{3,2,1,0:T(8,128)S(1)}, u32[]{:S(2)}, u32[]{:S(2)}) collective-permute-start(f32[3,2,18,32]{3,2,1,0:T(8,128)S(1)} %get-tuple-element.28), channel_id=1, source_target_pairs={{0,15},{1,0},{2,1},{3,2},{4,3},{5,4},{6,5},{7,6},{8,7},{9,8},{10,9... | collective-permute-start | bytes 41480 | tf_op jit(solution)/shard_map/ppermute | solution.py:16
  48.6 58.5 %copy-start.9 = (s32[4000]{0:T(1024)}, s32[4000]{0:T(1024)S(1)}, u32[]{:S(2)}) copy-start(s32[4000]{0:T(1024)S(1)} %reshape.254) | copy-start | bytes 48004
  49.9 10.4 %collective-permute-start.13 = (f32[3,2,18,32]{3,2,1,0:T(8,128)S(1)}, f32[3,2,18,32]{3,2,1,0:T(8,128)S(1)}, u32[]{:S(2)}, u32[]{:S(2)}) collective-permute-start(f32[3,2,18,32]{3,2,1,0:T(8,128)S(1)} %squeeze.122), channel_id=1, source_target_pairs={{0,16},{16,32},{32,48},{48,64},{64,80},{80,96},{96,112},{112,128},... | collective-permute-start | bytes 41480 | tf_op jit(solution)/shard_map/ppermute | solution.py:16
  58.4 9.0 %collective-permute-start.12 = (f32[3,2,18,32]{3,2,1,0:T(8,128)S(1)}, f32[3,2,18,32]{3,2,1,0:T(8,128)S(1)}, u32[]{:S(2)}, u32[]{:S(2)}) collective-permute-start(f32[3,2,18,32]{3,2,1,0:T(8,128)S(1)} %squeeze.122), channel_id=1, source_target_pairs={{0,496},{16,0},{32,16},{48,32},{64,48},{80,64},{96,80},{112,96},{1... | collective-permute-start | bytes 41480 | tf_op jit(solution)/shard_map/ppermute | solution.py:16
  67.4 14.5 %collective-permute-start.14 = (f32[3,2,18,32]{3,2,1,0:T(8,128)S(1)}, f32[3,2,18,32]{3,2,1,0:T(8,128)S(1)}, u32[]{:S(2)}, u32[]{:S(2)}) collective-permute-start(f32[3,2,18,32]{3,2,1,0:T(8,128)S(1)} %get-tuple-element.23), channel_id=1, source_target_pairs={{0,15},{1,0},{2,1},{3,2},{4,3},{5,4},{6,5},{7,6},{8,7},{9,8},{10,9... | collective-permute-start | bytes 41480 | tf_op jit(solution)/shard_map/ppermute | solution.py:16
  72.7 9.3 %collective-permute-start.15 = (f32[3,2,18,32]{3,2,1,0:T(8,128)S(1)}, f32[3,2,18,32]{3,2,1,0:T(8,128)S(1)}, u32[]{:S(2)}, u32[]{:S(2)}) collective-permute-start(f32[3,2,18,32]{3,2,1,0:T(8,128)S(1)} %get-tuple-element.24), channel_id=1, source_target_pairs={{0,1},{1,2},{2,3},{3,4},{4,5},{5,6},{6,7},{7,8},{8,9},{9,10},{10,1... | collective-permute-start | bytes 41480 | tf_op jit(solution)/shard_map/ppermute | solution.py:16
  75.5 9.4 %collective-permute-start.2 = (f32[3,32,128]{2,1,0:T(8,128)S(1)}, f32[3,32,128]{2,1,0:T(8,128)S(1)}, u32[]{:S(2)}, u32[]{:S(2)}) collective-permute-start(f32[3,32,128]{2,1,0:T(8,128)S(1)} %get-tuple-element.59), channel_id=1, source_target_pairs={{0,15},{1,0},{2,1},{3,2},{4,3},{5,4},{6,5},{7,6},{8,7},{9,8},{10,9... | collective-permute-start | bytes 147464 | tf_op jit(solution)/shard_map/ppermute | solution.py:16
  80.0 6.0 %collective-permute-start.3 = (f32[3,32,128]{2,1,0:T(8,128)S(1)}, f32[3,32,128]{2,1,0:T(8,128)S(1)}, u32[]{:S(2)}, u32[]{:S(2)}) collective-permute-start(f32[3,32,128]{2,1,0:T(8,128)S(1)} %get-tuple-element.60), channel_id=1, source_target_pairs={{0,1},{1,2},{2,3},{3,4},{4,5},{5,6},{6,7},{7,8},{8,9},{9,10},{10,1... | collective-permute-start | bytes 147464 | tf_op jit(solution)/shard_map/ppermute | solution.py:16
  82.8 3.4 copy-start.4
  100.7 2.9 copy-start.16
  130.4 5.9 %collective-permute-start.5 = (f32[3,32,128]{2,1,0:T(8,128)S(1)}, f32[3,32,128]{2,1,0:T(8,128)S(1)}, u32[]{:S(2)}, u32[]{:S(2)}) collective-permute-start(f32[3,32,128]{2,1,0:T(8,128)S(1)} %squeeze.117), channel_id=1, source_target_pairs={{0,16},{16,32},{32,48},{48,64},{64,80},{80,96},{96,112},{112,128},... | collective-permute-start | bytes 147464 | tf_op jit(solution)/shard_map/ppermute | solution.py:16
  134.2 8.7 %collective-permute-start.4 = (f32[3,32,128]{2,1,0:T(8,128)S(1)}, f32[3,32,128]{2,1,0:T(8,128)S(1)}, u32[]{:S(2)}, u32[]{:S(2)}) collective-permute-start(f32[3,32,128]{2,1,0:T(8,128)S(1)} %squeeze.116), channel_id=1, source_target_pairs={{0,496},{16,0},{32,16},{48,32},{64,48},{80,64},{96,80},{112,96},{1... | collective-permute-start | bytes 147464 | tf_op jit(solution)/shard_map/ppermute | solution.py:16
  143.0 5.5 %collective-permute-start.6 = (f32[3,32,128]{2,1,0:T(8,128)S(1)}, f32[3,32,128]{2,1,0:T(8,128)S(1)}, u32[]{:S(2)}, u32[]{:S(2)}) collective-permute-start(f32[3,32,128]{2,1,0:T(8,128)S(1)} %get-tuple-element.54), channel_id=1, source_target_pairs={{0,15},{1,0},{2,1},{3,2},{4,3},{5,4},{6,5},{7,6},{8,7},{9,8},{10,9... | collective-permute-start | bytes 147464 | tf_op jit(solution)/shard_map/ppermute | solution.py:16
  145.6 6.0 %collective-permute-start.7 = (f32[3,32,128]{2,1,0:T(8,128)S(1)}, f32[3,32,128]{2,1,0:T(8,128)S(1)}, u32[]{:S(2)}, u32[]{:S(2)}) collective-permute-start(f32[3,32,128]{2,1,0:T(8,128)S(1)} %get-tuple-element.55), channel_id=1, source_target_pairs={{0,1},{1,2},{2,3},{3,4},{4,5},{5,6},{6,7},{7,8},{8,9},{9,10},{10,1... | collective-permute-start | bytes 147464 | tf_op jit(solution)/shard_map/ppermute | solution.py:16
  196.4 72.1 %copy-start.1 = (f32[32,1280]{0,1:T(8,128)}, f32[32,1280]{0,1:T(8,128)S(1)}, u32[]{:S(2)}) copy-start(f32[32,1280]{0,1:T(8,128)S(1)} %broadcast_multiply_fusion) | copy-start | bytes 491524
  211.0 28.3 %copy-start.14 = (f32[2,18]{1,0:T(2,128)S(1)}, f32[2,18]{1,0:T(2,128)}, u32[]{:S(2)}) copy-start(f32[2,18]{1,0:T(2,128)} %param.17) | copy-start | bytes 436
  211.7 9.0 %collective-permute-start.24 = (f32[3,2,18,32]{3,2,1,0:T(8,128)S(1)}, f32[3,2,18,32]{3,2,1,0:T(8,128)S(1)}, u32[]{:S(2)}, u32[]{:S(2)}) collective-permute-start(f32[3,2,18,32]{3,2,1,0:T(8,128)S(1)} %get-tuple-element.20), channel_id=1, source_target_pairs={{0,496},{16,0},{32,16},{48,32},{64,48},{80,64},{96,80},{112,96},{1... | collective-permute-start | bytes 41480 | tf_op jit(solution)/shard_map/ppermute | solution.py:16
  213.6 8.4 %collective-permute-start.25 = (f32[3,2,18,32]{3,2,1,0:T(8,128)S(1)}, f32[3,2,18,32]{3,2,1,0:T(8,128)S(1)}, u32[]{:S(2)}, u32[]{:S(2)}) collective-permute-start(f32[3,2,18,32]{3,2,1,0:T(8,128)S(1)} %get-tuple-element.21), channel_id=1, source_target_pairs={{0,16},{16,32},{32,48},{48,64},{64,80},{80,96},{96,112},{112,128},... | collective-permute-start | bytes 41480 | tf_op jit(solution)/shard_map/ppermute | solution.py:16
  222.0 17.2 %collective-permute-start.27 = (f32[3,2,18,32]{3,2,1,0:T(8,128)S(1)}, f32[3,2,18,32]{3,2,1,0:T(8,128)S(1)}, u32[]{:S(2)}, u32[]{:S(2)}) collective-permute-start(f32[3,2,18,32]{3,2,1,0:T(8,128)S(1)} %get-tuple-element.18), channel_id=1, source_target_pairs={{0,1},{1,2},{2,3},{3,4},{4,5},{5,6},{6,7},{7,8},{8,9},{9,10},{10,1... | collective-permute-start | bytes 41480 | tf_op jit(solution)/shard_map/ppermute | solution.py:16
  223.9 15.3 %collective-permute-start.26 = (f32[3,2,18,32]{3,2,1,0:T(8,128)S(1)}, f32[3,2,18,32]{3,2,1,0:T(8,128)S(1)}, u32[]{:S(2)}, u32[]{:S(2)}) collective-permute-start(f32[3,2,18,32]{3,2,1,0:T(8,128)S(1)} %get-tuple-element.19), channel_id=1, source_target_pairs={{0,15},{1,0},{2,1},{3,2},{4,3},{5,4},{6,5},{7,6},{8,7},{9,8},{10,9... | collective-permute-start | bytes 41480 | tf_op jit(solution)/shard_map/ppermute | solution.py:16
  229.2 27.0 %collective-permute-start.16 = (f32[3,32,128]{2,1,0:T(8,128)}, f32[3,32,128]{2,1,0:T(8,128)S(1)}, u32[]{:S(2)}, u32[]{:S(2)}) collective-permute-start(f32[3,32,128]{2,1,0:T(8,128)} %get-tuple-element.74), channel_id=1, source_target_pairs={{0,496},{16,0},{32,16},{48,32},{64,48},{80,64},{96,80},{112,96},{1... | collective-permute-start | bytes 147464 | tf_op jit(solution)/shard_map/ppermute | solution.py:16
  231.1 25.1 %collective-permute-start.17 = (f32[3,32,128]{2,1,0:T(8,128)}, f32[3,32,128]{2,1,0:T(8,128)S(1)}, u32[]{:S(2)}, u32[]{:S(2)}) collective-permute-start(f32[3,32,128]{2,1,0:T(8,128)} %get-tuple-element.75), channel_id=1, source_target_pairs={{0,16},{16,32},{32,48},{48,64},{64,80},{80,96},{96,112},{112,128},... | collective-permute-start | bytes 147464 | tf_op jit(solution)/shard_map/ppermute | solution.py:16
  239.4 4.4 collective-permute-start.29
  241.8 9.0 %collective-permute-start.28 = (f32[3,2,18,32]{3,2,1,0:T(8,128)S(1)}, f32[3,2,18,32]{3,2,1,0:T(8,128)S(1)}, u32[]{:S(2)}, u32[]{:S(2)}) collective-permute-start(f32[3,2,18,32]{3,2,1,0:T(8,128)S(1)} %squeeze.133), channel_id=1, source_target_pairs={{0,496},{16,0},{32,16},{48,32},{64,48},{80,64},{96,80},{112,96},{1... | collective-permute-start | bytes 41480 | tf_op jit(solution)/shard_map/ppermute | solution.py:16
  250.9 11.3 %collective-permute-start.30 = (f32[3,2,18,32]{3,2,1,0:T(8,128)S(1)}, f32[3,2,18,32]{3,2,1,0:T(8,128)S(1)}, u32[]{:S(2)}, u32[]{:S(2)}) collective-permute-start(f32[3,2,18,32]{3,2,1,0:T(8,128)S(1)} %get-tuple-element.14), channel_id=1, source_target_pairs={{0,15},{1,0},{2,1},{3,2},{4,3},{5,4},{6,5},{7,6},{8,7},{9,8},{10,9... | collective-permute-start | bytes 41480 | tf_op jit(solution)/shard_map/ppermute | solution.py:16
  253.0 9.1 %collective-permute-start.31 = (f32[3,2,18,32]{3,2,1,0:T(8,128)S(1)}, f32[3,2,18,32]{3,2,1,0:T(8,128)S(1)}, u32[]{:S(2)}, u32[]{:S(2)}) collective-permute-start(f32[3,2,18,32]{3,2,1,0:T(8,128)S(1)} %get-tuple-element.15), channel_id=1, source_target_pairs={{0,1},{1,2},{2,3},{3,4},{4,5},{5,6},{6,7},{7,8},{8,9},{9,10},{10,1... | collective-permute-start | bytes 41480 | tf_op jit(solution)/shard_map/ppermute | solution.py:16
  256.8 8.2 %collective-permute-start.18 = (f32[3,32,128]{2,1,0:T(8,128)}, f32[3,32,128]{2,1,0:T(8,128)}, u32[]{:S(2)}, u32[]{:S(2)}) collective-permute-start(f32[3,32,128]{2,1,0:T(8,128)} %get-tuple-element.49), channel_id=1, source_target_pairs={{0,15},{1,0},{2,1},{3,2},{4,3},{5,4},{6,5},{7,6},{8,7},{9,8},{10,9... | collective-permute-start | bytes 147464 | tf_op jit(solution)/shard_map/ppermute | solution.py:16
  260.2 6.4 %collective-permute-start.19 = (f32[3,32,128]{2,1,0:T(8,128)}, f32[3,32,128]{2,1,0:T(8,128)}, u32[]{:S(2)}, u32[]{:S(2)}) collective-permute-start(f32[3,32,128]{2,1,0:T(8,128)} %get-tuple-element.50), channel_id=1, source_target_pairs={{0,1},{1,2},{2,3},{3,4},{4,5},{5,6},{6,7},{7,8},{8,9},{9,10},{10,1... | collective-permute-start | bytes 147464 | tf_op jit(solution)/shard_map/ppermute | solution.py:16
  283.7 2.9 copy-start.17
  313.1 15.1 %copy-start.3 = (f32[32,2304]{0,1:T(8,128)}, f32[32,2304]{0,1:T(8,128)S(1)}, u32[]{:S(2)}) copy-start(f32[32,2304]{0,1:T(8,128)S(1)} %scatter_custom_fusion.3) | copy-start | bytes 884740
  313.4 5.9 %collective-permute-start.21 = (f32[3,32,128]{2,1,0:T(8,128)S(1)}, f32[3,32,128]{2,1,0:T(8,128)S(1)}, u32[]{:S(2)}, u32[]{:S(2)}) collective-permute-start(f32[3,32,128]{2,1,0:T(8,128)S(1)} %squeeze.128), channel_id=1, source_target_pairs={{0,16},{16,32},{32,48},{48,64},{64,80},{80,96},{96,112},{112,128},... | collective-permute-start | bytes 147464 | tf_op jit(solution)/shard_map/ppermute | solution.py:16
  317.3 8.7 %collective-permute-start.20 = (f32[3,32,128]{2,1,0:T(8,128)S(1)}, f32[3,32,128]{2,1,0:T(8,128)S(1)}, u32[]{:S(2)}, u32[]{:S(2)}) collective-permute-start(f32[3,32,128]{2,1,0:T(8,128)S(1)} %squeeze.127), channel_id=1, source_target_pairs={{0,496},{16,0},{32,16},{48,32},{64,48},{80,64},{96,80},{112,96},{1... | collective-permute-start | bytes 147464 | tf_op jit(solution)/shard_map/ppermute | solution.py:16
  326.0 6.7 %collective-permute-start.22 = (f32[3,32,128]{2,1,0:T(8,128)S(1)}, f32[3,32,128]{2,1,0:T(8,128)S(1)}, u32[]{:S(2)}, u32[]{:S(2)}) collective-permute-start(f32[3,32,128]{2,1,0:T(8,128)S(1)} %get-tuple-element.44), channel_id=1, source_target_pairs={{0,15},{1,0},{2,1},{3,2},{4,3},{5,4},{6,5},{7,6},{8,7},{9,8},{10,9... | collective-permute-start | bytes 147464 | tf_op jit(solution)/shard_map/ppermute | solution.py:16
  328.2 6.0 %collective-permute-start.23 = (f32[3,32,128]{2,1,0:T(8,128)S(1)}, f32[3,32,128]{2,1,0:T(8,128)S(1)}, u32[]{:S(2)}, u32[]{:S(2)}) collective-permute-start(f32[3,32,128]{2,1,0:T(8,128)S(1)} %get-tuple-element.45), channel_id=1, source_target_pairs={{0,1},{1,2},{2,3},{3,4},{4,5},{5,6},{6,7},{7,8},{8,9},{9,10},{10,1... | collective-permute-start | bytes 147464 | tf_op jit(solution)/shard_map/ppermute | solution.py:16
  381.4 27.7 %copy-start.15 = (f32[2,18]{1,0:T(2,128)S(1)}, f32[2,18]{1,0:T(2,128)}, u32[]{:S(2)}) copy-start(f32[2,18]{1,0:T(2,128)} %param.17) | copy-start | bytes 436
  382.1 9.0 %collective-permute-start.40 = (f32[3,2,18,32]{3,2,1,0:T(8,128)S(1)}, f32[3,2,18,32]{3,2,1,0:T(8,128)S(1)}, u32[]{:S(2)}, u32[]{:S(2)}) collective-permute-start(f32[3,2,18,32]{3,2,1,0:T(8,128)S(1)} %get-tuple-element.11), channel_id=1, source_target_pairs={{0,496},{16,0},{32,16},{48,32},{64,48},{80,64},{96,80},{112,96},{1... | collective-permute-start | bytes 41480 | tf_op jit(solution)/shard_map/ppermute | solution.py:16
  384.1 8.4 %collective-permute-start.41 = (f32[3,2,18,32]{3,2,1,0:T(8,128)S(1)}, f32[3,2,18,32]{3,2,1,0:T(8,128)S(1)}, u32[]{:S(2)}, u32[]{:S(2)}) collective-permute-start(f32[3,2,18,32]{3,2,1,0:T(8,128)S(1)} %get-tuple-element.12), channel_id=1, source_target_pairs={{0,16},{16,32},{32,48},{48,64},{64,80},{80,96},{96,112},{112,128},... | collective-permute-start | bytes 41480 | tf_op jit(solution)/shard_map/ppermute | solution.py:16
  392.5 16.6 %collective-permute-start.43 = (f32[3,2,18,32]{3,2,1,0:T(8,128)S(1)}, f32[3,2,18,32]{3,2,1,0:T(8,128)S(1)}, u32[]{:S(2)}, u32[]{:S(2)}) collective-permute-start(f32[3,2,18,32]{3,2,1,0:T(8,128)S(1)} %get-tuple-element.9), channel_id=1, source_target_pairs={{0,1},{1,2},{2,3},{3,4},{4,5},{5,6},{6,7},{7,8},{8,9},{9,10},{10,1... | collective-permute-start | bytes 41480 | tf_op jit(solution)/shard_map/ppermute | solution.py:16
  394.4 14.7 %collective-permute-start.42 = (f32[3,2,18,32]{3,2,1,0:T(8,128)S(1)}, f32[3,2,18,32]{3,2,1,0:T(8,128)S(1)}, u32[]{:S(2)}, u32[]{:S(2)}) collective-permute-start(f32[3,2,18,32]{3,2,1,0:T(8,128)S(1)} %get-tuple-element.10), channel_id=1, source_target_pairs={{0,15},{1,0},{2,1},{3,2},{4,3},{5,4},{6,5},{7,6},{8,7},{9,8},{10,9... | collective-permute-start | bytes 41480 | tf_op jit(solution)/shard_map/ppermute | solution.py:16
  399.0 27.0 %collective-permute-start.32 = (f32[3,32,128]{2,1,0:T(8,128)S(1)}, f32[3,32,128]{2,1,0:T(8,128)S(1)}, u32[]{:S(2)}, u32[]{:S(2)}) collective-permute-start(f32[3,32,128]{2,1,0:T(8,128)S(1)} %get-tuple-element.66), channel_id=1, source_target_pairs={{0,496},{16,0},{32,16},{48,32},{64,48},{80,64},{96,80},{112,96},{1... | collective-permute-start | bytes 147464 | tf_op jit(solution)/shard_map/ppermute | solution.py:16
  400.9 25.1 %collective-permute-start.33 = (f32[3,32,128]{2,1,0:T(8,128)S(1)}, f32[3,32,128]{2,1,0:T(8,128)S(1)}, u32[]{:S(2)}, u32[]{:S(2)}) collective-permute-start(f32[3,32,128]{2,1,0:T(8,128)S(1)} %get-tuple-element.67), channel_id=1, source_target_pairs={{0,16},{16,32},{32,48},{48,64},{64,80},{80,96},{96,112},{112,128},... | collective-permute-start | bytes 147464 | tf_op jit(solution)/shard_map/ppermute | solution.py:16
  409.3 4.4 collective-permute-start.45
  411.7 9.0 %collective-permute-start.44 = (f32[3,2,18,32]{3,2,1,0:T(8,128)S(1)}, f32[3,2,18,32]{3,2,1,0:T(8,128)S(1)}, u32[]{:S(2)}, u32[]{:S(2)}) collective-permute-start(f32[3,2,18,32]{3,2,1,0:T(8,128)S(1)} %squeeze.144), channel_id=1, source_target_pairs={{0,496},{16,0},{32,16},{48,32},{64,48},{80,64},{96,80},{112,96},{1... | collective-permute-start | bytes 41480 | tf_op jit(solution)/shard_map/ppermute | solution.py:16
  420.7 11.3 %collective-permute-start.46 = (f32[3,2,18,32]{3,2,1,0:T(8,128)S(1)}, f32[3,2,18,32]{3,2,1,0:T(8,128)S(1)}, u32[]{:S(2)}, u32[]{:S(2)}) collective-permute-start(f32[3,2,18,32]{3,2,1,0:T(8,128)S(1)} %get-tuple-element.5), channel_id=1, source_target_pairs={{0,15},{1,0},{2,1},{3,2},{4,3},{5,4},{6,5},{7,6},{8,7},{9,8},{10,9... | collective-permute-start | bytes 41480 | tf_op jit(solution)/shard_map/ppermute | solution.py:16
  423.5 8.5 %collective-permute-start.47 = (f32[3,2,18,32]{3,2,1,0:T(8,128)S(1)}, f32[3,2,18,32]{3,2,1,0:T(8,128)S(1)}, u32[]{:S(2)}, u32[]{:S(2)}) collective-permute-start(f32[3,2,18,32]{3,2,1,0:T(8,128)S(1)} %get-tuple-element.6), channel_id=1, source_target_pairs={{0,1},{1,2},{2,3},{3,4},{4,5},{5,6},{6,7},{7,8},{8,9},{9,10},{10,1... | collective-permute-start | bytes 41480 | tf_op jit(solution)/shard_map/ppermute | solution.py:16
  426.1 8.8 %collective-permute-start.34 = (f32[3,32,128]{2,1,0:T(8,128)S(1)}, f32[3,32,128]{2,1,0:T(8,128)S(1)}, u32[]{:S(2)}, u32[]{:S(2)}) collective-permute-start(f32[3,32,128]{2,1,0:T(8,128)S(1)} %get-tuple-element.39), channel_id=1, source_target_pairs={{0,15},{1,0},{2,1},{3,2},{4,3},{5,4},{6,5},{7,6},{8,7},{9,8},{10,9... | collective-permute-start | bytes 147464 | tf_op jit(solution)/shard_map/ppermute | solution.py:16
  430.1 6.0 %collective-permute-start.35 = (f32[3,32,128]{2,1,0:T(8,128)S(1)}, f32[3,32,128]{2,1,0:T(8,128)S(1)}, u32[]{:S(2)}, u32[]{:S(2)}) collective-permute-start(f32[3,32,128]{2,1,0:T(8,128)S(1)} %get-tuple-element.40), channel_id=1, source_target_pairs={{0,1},{1,2},{2,3},{3,4},{4,5},{5,6},{6,7},{7,8},{8,9},{9,10},{10,1... | collective-permute-start | bytes 147464 | tf_op jit(solution)/shard_map/ppermute | solution.py:16
  450.6 2.9 copy-start.18
  480.3 5.9 %collective-permute-start.37 = (f32[3,32,128]{2,1,0:T(8,128)S(1)}, f32[3,32,128]{2,1,0:T(8,128)S(1)}, u32[]{:S(2)}, u32[]{:S(2)}) collective-permute-start(f32[3,32,128]{2,1,0:T(8,128)S(1)} %squeeze.139), channel_id=1, source_target_pairs={{0,16},{16,32},{32,48},{48,64},{64,80},{80,96},{96,112},{112,128},... | collective-permute-start | bytes 147464 | tf_op jit(solution)/shard_map/ppermute | solution.py:16
  484.1 8.7 %collective-permute-start.36 = (f32[3,32,128]{2,1,0:T(8,128)S(1)}, f32[3,32,128]{2,1,0:T(8,128)S(1)}, u32[]{:S(2)}, u32[]{:S(2)}) collective-permute-start(f32[3,32,128]{2,1,0:T(8,128)S(1)} %squeeze.138), channel_id=1, source_target_pairs={{0,496},{16,0},{32,16},{48,32},{64,48},{80,64},{96,80},{112,96},{1... | collective-permute-start | bytes 147464 | tf_op jit(solution)/shard_map/ppermute | solution.py:16
  492.9 5.5 %collective-permute-start.38 = (f32[3,32,128]{2,1,0:T(8,128)S(1)}, f32[3,32,128]{2,1,0:T(8,128)S(1)}, u32[]{:S(2)}, u32[]{:S(2)}) collective-permute-start(f32[3,32,128]{2,1,0:T(8,128)S(1)} %get-tuple-element.34), channel_id=1, source_target_pairs={{0,15},{1,0},{2,1},{3,2},{4,3},{5,4},{6,5},{7,6},{8,7},{9,8},{10,9... | collective-permute-start | bytes 147464 | tf_op jit(solution)/shard_map/ppermute | solution.py:16
  495.4 6.0 %collective-permute-start.39 = (f32[3,32,128]{2,1,0:T(8,128)S(1)}, f32[3,32,128]{2,1,0:T(8,128)S(1)}, u32[]{:S(2)}, u32[]{:S(2)}) collective-permute-start(f32[3,32,128]{2,1,0:T(8,128)S(1)} %get-tuple-element.35), channel_id=1, source_target_pairs={{0,1},{1,2},{2,3},{3,4},{4,5},{5,6},{6,7},{7,8},{8,9},{9,10},{10,1... | collective-permute-start | bytes 147464 | tf_op jit(solution)/shard_map/ppermute | solution.py:16
  508.3 25.7 %copy-start.2 = (f32[32,1280]{0,1:T(8,128)S(1)}, f32[32,1280]{0,1:T(8,128)}, u32[]{:S(2)}) copy-start(f32[32,1280]{0,1:T(8,128)} %copy-done.1) | copy-start | bytes 491524
  (3 other events, 8.6 us)
where the time goes:
time: 545 us; the launch traced here: 535 us
  other arithmetic  185 us (34%)
  starting transfers between devices  169 us (31%)
  local copies, waits for them, and re-layouts  115 us (21%)
  waiting for transfers between devices  57.2 us (10%)
  matrix products  7.02 us (1%)
    ppermute x48, starting transfers between devices, passed_along(): return lax.ppermute(value, axis, pairs)  169 us
    scatter-add x3, other arithmetic, apply(): own = own.at[:, proj_nodes].add(added)  77.1 us
    scatter-add x3, other arithmetic, apply(): assembled = jnp.zeros_like(extended).at[:, cell_nodes].add(product)  69 us
    ppermute x48, waiting for transfers between devices, passed_along(): return lax.ppermute(value, axis, pairs)  57.2 us
    gather x6, local copies, waits for them, and re-layouts, apply(): cellv = extended[:, cell_nodes]  51.1 us
    gather x6, local copies, waits for them, and re-layouts, apply(): gathered = field[:, proj_nodes]  32 us
    scatter-add x3, other arithmetic, apply(): own = own.at[:, send_nodes].add(without_center(back).transpose(1, 0, 2))  31.6 us
  transfers between devices with their start and end apart: 48, of which 18 were waited for; matrix products, arithmetic and copies ran while one was open for 5% of the time, Pallas kernels for 0%

commit v1 on v0

v1 whole, which is shorter than its diff:
```python
import functools

import jax
import jax.numpy as jnp
from jax import lax
from jax.experimental import pallas as pl
from jax.experimental.pallas import tpu as pltpu
from jax.sharding import PartitionSpec as P

DEGREES = 3
CHEB_CENTER = 5.0
CHEB_HALF = 6.0
MESH = pl.DeviceIdType.MESH
OFFS = ((-1, -1), (-1, 0), (-1, 1), (0, -1), (0, 1), (1, -1), (1, 0), (1, 1))

VEC = 32
NODE = 1280
OWN = 5
GHO = 4
LO = 256
CN = 125
CELLS = 32
SLOTS = CELLS * 128
SENDS = 1024
PRO = 18
PPAD = 24
PK = 2 * PPAD
PALL = 9 * PK
BF = jnp.bfloat16
F32 = jnp.float32


def split(x):
    hi = x.astype(BF)
    return hi, (x - hi.astype(F32)).astype(BF)


def dot(a, b):
    return jnp.dot(a, b, preferred_element_type=F32)


def dot_nt(a, b):
    return lax.dot_general(a, b, (((1,), (1,)), ((), ())), preferred_element_type=F32)


def lanes(j, width):
    return pl.ds(pl.multiple_of(j * width, width), width)


def kernel(
    nx, ny,
    block, pot, cnodes, stiff, sends, pnodes, pvals, coup, cscale,
    out,
    field, prev, own, cellown, flhs, glhs, klhs, slhs, blhs, eall,
    ci, ct, ohg, hi8, mb, ohs, ohsend, shi8, smb, ohb, wf, whi, wlo, kmat, crow, cslab,
    sva, rva, svb, rvb,
    sema, sema_r, semb, semb_r,
):
    ix = lax.axis_index("mx")
    iy = lax.axis_index("my")

    def at(ox, oy):
        return (lax.rem(ix + ox + nx, nx), lax.rem(iy + oy + ny, ny))

    barrier = pltpu.get_barrier_semaphore()
    for ox, oy in OFFS:
        pl.semaphore_signal(barrier, inc=1, device_id=at(ox, oy), device_id_type=MESH)

    ci[...] = jnp.full((128, 128), -1, jnp.int32)
    ci[0:CN, 0:CELLS] = cnodes[...]
    ct[...] = ci[...].T
    sub = lax.broadcasted_iota(jnp.int32, (LO, 128), 0)

    def cell_tables(c, carry):
        at_c = lanes(c, 128)
        row = ct[pl.ds(c, 1), :]
        hot = jnp.where(sub == (row & (LO - 1)), 1.0, 0.0).astype(BF)
        ohg[0:LO, at_c] = hot
        ohg[LO:2 * LO, at_c] = hot
        high = jnp.broadcast_to(row >> 8, (16, 128))
        hi8[:, at_c] = high[0:8]
        for th in range(OWN + GHO):
            mb[th, :, at_c] = jnp.where(high == th, 1.0, 0.0).astype(BF)
        return carry

    lax.fori_loop(0, CELLS, cell_tables, 0)

    for k in range(8):
        at_k = slice(k * 128, (k + 1) * 128)
        row = sends[k:k + 1, :]
        hot = jnp.where(sub == (row & (LO - 1)), 1.0, 0.0).astype(BF)
        ohsend[0:LO, at_k] = hot
        ohsend[LO:2 * LO, at_k] = hot
        high = jnp.broadcast_to(row >> 8, (16, 128))
        shi8[:, at_k] = high[0:8]
        for th in range(OWN):
            smb[th, :, at_k] = jnp.where(high == th, 1.0, 0.0).astype(BF)

    wf[...] = jnp.zeros_like(wf)
    sub2 = lax.broadcasted_iota(jnp.int32, (LO, LO), 0)
    for k in range(9):
        for a in range(2):
            row = pnodes[k, a:a + 1, :]
            hot = jnp.where(sub2 == (row & (LO - 1)), 1.0, 0.0).astype(BF)
            high = jnp.broadcast_to(row >> 8, (PRO, LO))
            vhi, vlo = split(pvals[k, a])
            vhi = vhi.astype(F32)
            vlo = vlo.astype(F32)
            base = (2 * k + a) * PPAD
            for th in range(OWN):
                m = high == th
                got = dot_nt(jnp.where(m, vhi, 0.0).astype(BF), hot) + dot_nt(jnp.where(m, vlo, 0.0).astype(BF), hot)
                wf[base:base + PRO, th * LO:(th + 1) * LO] = got
    for k in range(9):
        hi, lo = split(wf[k * PK:(k + 1) * PK, :])
        whi[k * PK:(k + 1) * PK, :] = hi
        wlo[k * PK:(k + 1) * PK, :] = lo

    kf = own.at[:, 0:128]
    wf[0:128, 0:128] = jnp.zeros((128, 128), F32)
    wf[0:CN, 0:CN] = stiff[...]
    khi, klo = split(wf[0:128, 0:128])
    for r in range(2):
        kmat[r * 128:(r + 1) * 128, 0:128] = khi
        kmat[r * 128:(r + 1) * 128, 128:256] = klo

    crow[...] = jnp.zeros_like(crow)
    for h in range(2):
        for a in range(2):
            start = 64 * h + PPAD * a
            crow[0:1, start:start + PRO] = coup[a:a + 1, :]
    for m in range(DEGREES):
        for k in range(8):
            sva[m, k, VEC:VEC + 16, :] = jnp.zeros((16, 128), F32)
    cslab[...] = jnp.zeros_like(cslab)

    field[...] = block[...]
    prev[...] = jnp.zeros_like(prev)

    def apply(m, carry):
        f = field[...]
        for th in range(OWN):
            hi, lo = split(f[:, th * LO:(th + 1) * LO])
            flhs[th * VEC:(th + 1) * VEC, 0:LO] = hi
            flhs[th * VEC:(th + 1) * VEC, LO:2 * LO] = lo

        for j in range(4):
            at_j = slice(j * LO, (j + 1) * LO)
            got = dot(flhs[...], ohsend[:, at_j])
            high = shi8[0:1, at_j]
            acc = got[0:VEC]
            for th in range(1, OWN):
                acc = jnp.where(high == th, got[th * VEC:(th + 1) * VEC], acc)
            sva[m, 2 * j, 0:VEC, :] = acc[:, 0:128]
            sva[m, 2 * j + 1, 0:VEC, :] = acc[:, 128:256]
        fhi, flo = split(f)
        c = dot_nt(fhi, whi[...]) + dot_nt(flo, whi[...]) + dot_nt(fhi, wlo[...])
        for k in range(9):
            piece = c[:, k * PK:(k + 1) * PK]
            if k == 4:
                cslab[:, 0:PK] = piece[0:16]
                cslab[:, 64:64 + PK] = piece[16:32]
            else:
                d = k if k < 4 else k - 1
                sva[m, d, VEC:VEC + 16, 0:PK] = piece[0:16]
                sva[m, d, VEC:VEC + 16, 64:64 + PK] = piece[16:32]

        @pl.when(m == 0)
        def _():
            pl.semaphore_wait(barrier, 8)

        def copy_a(k):
            return pltpu.make_async_remote_copy(
                src_ref=sva.at[m, k], dst_ref=rva.at[m, k],
                send_sem=sema.at[m, k], recv_sem=sema_r.at[m, k],
                device_id=at(*OFFS[k]), device_id_type=MESH,
            )

        def copy_b(k):
            return pltpu.make_async_remote_copy(
                src_ref=svb.at[m, k], dst_ref=rvb.at[m, k],
                send_sem=semb.at[m, k], recv_sem=semb_r.at[m, k],
                device_id=at(-OFFS[k][0], -OFFS[k][1]), device_id_type=MESH,
            )

        for k in range(8):
            copy_a(k).start()

        def gather_own(j, carry):
            at_j = lanes(j, LO)
            got = dot(flhs[...], ohg[:, at_j])
            high = hi8[0:1, at_j]
            acc = jnp.where(high == 0, got[0:VEC], 0.0)
            for th in range(1, OWN):
                acc = jnp.where(high == th, got[th * VEC:(th + 1) * VEC], acc)
            cellown[:, at_j] = acc
            return carry

        lax.fori_loop(0, SLOTS // LO, gather_own, 0)

        for k in range(8):
            copy_a(k).wait_recv()
        for k in range(8):
            hi, lo = split(rva[m, k, 0:VEC, :])
            t, h = k // 2, (k % 2) * 128
            glhs[t * VEC:(t + 1) * VEC, h:h + 128] = hi
            glhs[t * VEC:(t + 1) * VEC, LO + h:LO + h + 128] = lo

        def gather_ghost(j, carry):
            at_j = lanes(j, LO)
            got = dot(glhs[...], ohg[:, at_j])
            high = hi8[0:1, at_j]
            acc = cellown[:, at_j]
            for th in range(GHO):
                acc = jnp.where(high == OWN + th, got[th * VEC:(th + 1) * VEC], acc)
            hi, lo = split(acc)
            for h in range(2):
                rows = pl.ds(pl.multiple_of(j * 2 * VEC, 2 * VEC) + h * VEC, VEC)
                klhs[rows, 0:128] = hi[:, h * 128:(h + 1) * 128]
                klhs[rows, 128:256] = lo[:, h * 128:(h + 1) * 128]
            return carry

        lax.fori_loop(0, SLOTS // LO, gather_ghost, 0)

        def products(j, carry):
            got = dot(klhs[lanes(j, 256), :], kmat[...])
            prod = got[:, 0:128] + got[:, 128:256]
            for i in range(8):
                at_c = pl.ds(pl.multiple_of(j * 1024, 1024) + i * 128, 128)
                hi, lo = split(prod[i * VEC:(i + 1) * VEC] * cscale[j * 8 + i])
                for th in range(OWN + GHO):
                    mask = mb[th, :, at_c]
                    base = th * 2 * VEC
                    for r in range(2):
                        slhs[base + 16 * r:base + 16 * r + 16, at_c] = hi[16 * r:16 * r + 16] * mask
                        slhs[base + VEC + 16 * r:base + VEC + 16 * r + 16, at_c] = lo[16 * r:16 * r + 16] * mask
            return carry

        lax.fori_loop(0, CELLS // 8, products, 0)

        got = dot_nt(slhs[OWN * 2 * VEC:(OWN + GHO) * 2 * VEC, :], ohg[0:LO, :])
        for t in range(GHO):
            both = got[t * 2 * VEC:t * 2 * VEC + VEC] + got[t * 2 * VEC + VEC:(t + 1) * 2 * VEC]
            svb[m, 2 * t, 0:VEC, :] = both[:, 0:128]
            svb[m, 2 * t + 1, 0:VEC, :] = both[:, 128:256]
        total = cslab[...]
        for k in range(8):
            total = total + rva[m, k, VEC:VEC + 16, :]
        coef = total * crow[0:1, :]
        for k in range(8):
            svb[m, k, VEC:VEC + 16, :] = coef
            copy_b(k).start()

        f = field[...]
        got = dot_nt(slhs[0:OWN * 2 * VEC, :], ohg[0:LO, :])
        base = (pot[...] - CHEB_CENTER) * f
        for th in range(OWN):
            at_t = slice(th * LO, (th + 1) * LO)
            both = got[th * 2 * VEC:th * 2 * VEC + VEC] + got[th * 2 * VEC + VEC:(th + 1) * 2 * VEC]
            own[:, at_t] = both + base[:, at_t]

        for k in range(8):
            copy_b(k).wait_recv()
        for k in range(8):
            at_k = slice(k * 128, (k + 1) * 128)
            hi, lo = split(rvb[m, k, 0:VEC, :])
            for th in range(OWN):
                mask = smb[th, :, at_k]
                row = th * 2 * VEC
                for r in range(2):
                    blhs[row + 16 * r:row + 16 * r + 16, at_k] = hi[16 * r:16 * r + 16] * mask
                    blhs[row + VEC + 16 * r:row + VEC + 16 * r + 16, at_k] = lo[16 * r:16 * r + 16] * mask
        for k in range(9):
            if k == 4:
                slab = coef
            else:
                slab = rvb[m, k if k < 4 else k - 1, VEC:VEC + 16, :]
            eall[0:16, k * PK:(k + 1) * PK] = slab[:, 0:PK]
            eall[16:32, k * PK:(k + 1) * PK] = slab[:, 64:64 + PK]
        ehi, elo = split(eall[...])
        spread = dot(ehi, whi[...]) + dot(elo, whi[...]) + dot(ehi, wlo[...])
        got = dot_nt(blhs[...], ohsend[0:LO, :])
        alpha = jnp.where(m == 0, 1.0 / CHEB_HALF, 2.0 / CHEB_HALF)
        for th in range(OWN):
            at_t = slice(th * LO, (th + 1) * LO)
            both = got[th * 2 * VEC:th * 2 * VEC + VEC] + got[th * 2 * VEC + VEC:(th + 1) * 2 * VEC]
            new = alpha * (own[:, at_t] + both + spread[:, at_t]) - prev[:, at_t]
            prev[:, at_t] = field[:, at_t]
            field[:, at_t] = new
        for k in range(8):
            copy_a(k).wait_send()
            copy_b(k).wait_send()
        return carry

    lax.fori_loop(0, DEGREES, apply, 0)
    out[...] = field[...]


def shards(block, potential, cell_nodes, cell_scale, stiffness, send_nodes, proj_nodes, proj_values, coupling):
    nx, ny = lax.axis_size("mx"), lax.axis_size("my")
    vmem = pl.BlockSpec(memory_space=pltpu.VMEM)
    smem = pl.BlockSpec(memory_space=pltpu.SMEM)
    msg = pltpu.VMEM((DEGREES, 8, VEC + 16, 128), F32)
    sem = pltpu.SemaphoreType.DMA((DEGREES, 8))
    return pl.pallas_call(
        functools.partial(kernel, nx, ny),
        out_shape=jax.ShapeDtypeStruct((VEC, NODE), F32),
        in_specs=[vmem] * 8 + [smem],
        out_specs=vmem,
        scratch_shapes=[
            pltpu.VMEM((VEC, NODE), F32),
            pltpu.VMEM((VEC, NODE), F32),
            pltpu.VMEM((VEC, NODE), F32),
            pltpu.VMEM((VEC, SLOTS), F32),
            pltpu.VMEM((OWN * VEC, 2 * LO), BF),
            pltpu.VMEM((GHO * VEC, 2 * LO), BF),
            pltpu.VMEM((CELLS * VEC, 256), BF),
            pltpu.VMEM(((OWN + GHO) * 2 * VEC, SLOTS), BF),
            pltpu.VMEM((OWN * 2 * VEC, SENDS), BF),
            pltpu.VMEM((VEC, PALL), F32),
            pltpu.VMEM((128, 128), jnp.int32),
            pltpu.VMEM((128, 128), jnp.int32),
            pltpu.VMEM((2 * LO, SLOTS), BF),
            pltpu.VMEM((8, SLOTS), jnp.int32),
            pltpu.VMEM((OWN + GHO, 16, SLOTS), BF),
            pltpu.VMEM((16, 128), BF),
            pltpu.VMEM((2 * LO, SENDS), BF),
            pltpu.VMEM((8, SENDS), jnp.int32),
            pltpu.VMEM((OWN, 16, SENDS), BF),
            pltpu.VMEM((16, 128), BF),
            pltpu.VMEM((PALL, NODE), F32),
            pltpu.VMEM((PALL, NODE), BF),
            pltpu.VMEM((PALL, NODE), BF),
            pltpu.VMEM((256, 256), BF),
            pltpu.VMEM((8, 128), F32),
            pltpu.VMEM((16, 128), F32),
            msg, msg, msg, msg,
            sem, sem, sem, sem,
        ],
        compiler_params=pltpu.CompilerParams(
            collective_id=0, has_side_effects=True, vmem_limit_bytes=48 * 1024 * 1024
        ),
        name="filtered",
    )(block, potential.reshape(1, NODE), cell_nodes, stiffness, send_nodes, proj_nodes, proj_values, coupling, cell_scale)


def solution(mesh):
    both = ("mx", "my")
    placed = (
        P(None, both), P(both), P(None, both), P(both), P(), P(None, both),
        P(None, both, None), P(None, both, None, None), P(both, None),
    )
    return jax.shard_map(shards, mesh=mesh, in_specs=placed, out_specs=P(None, both), check_vma=False)
```

time: 545 us -> 85.2 us (0.16)
  the two profiles are of different devices: /device:TPU:31 before, /device:TPU:1 now
where the time goes in v1:
time: 85.2 us; the launch traced here: 84.9 us
  Pallas kernels  81.5 us (96%)
  local copies, waits for them, and re-layouts  3.35 us (4%)
    pallas_call x1, Pallas kernels, shards(): pl.pallas_call(functools.partial(kernel, nx, ny), out_shape=jax.ShapeDtyp...  81.5 us
    unnamed x15, local copies, waits for them, and re-layouts  2.65 us

profile of v1, /device:TPU:1, one launch (start us, length us, event | category | flops | bytes accessed | tf_op | source)
XLA Modules:
  0.0 84.9 jit_solution(7956940578311958758)
XLA Ops:
  0.0 0.7 reshape.3.pot
  0.7 0.8 copy.10.cnodes
  1.5 0.0 copy-start
  1.5 0.0 copy-start.1
  1.5 0.0 copy-start.2
  1.6 0.0 copy-start.3
  1.6 0.0 copy-start.4
  1.6 0.0 copy-start.5
  1.6 1.1 %copy.11.pvals = f32[9,2,18,256]{3,2,1,0:T(8,128)S(1)} copy(f32[9,2,18,256]{3,1,2,0:T(2,128)} %param.16) | data formatting | bytes 663552 | tf_op args[7]
  2.7 0.0 copy-done
  2.7 0.0 copy-done.1
  2.7 0.0 copy-done.2
  2.8 0.0 copy-done.3
  2.8 0.0 copy-done.4
  2.8 0.0 copy-done.5
  2.8 81.5 %filtered.1 = f32[32,1280]{1,0:T(8,128)S(1)} custom-call(f32[32,1280]{1,0:T(8,128)S(1)} %copy-done, f32[1,1280]{1,0:T(1,128)S(1)} %reshape.3.pot, s32[125,32]{1,0:T(8,128)S(1)} %copy.10.cnodes, f32[125,125]{1,0:T(8,128)S(1)} %copy-done.1, s32[8,128]{1,0:T(8,128)S(1)} %copy-done.3, s32[9,2,256]{2,1,0:T(2,128)S(1)} %copy-done.2, ...), custom_call_target="tpu_custom_call" | custom-call | tf_op jit(solution)/shard_map/filtered/pallas_call | solution.py:305
  84.2 0.7 copy.13
Async XLA Ops:
  1.5 1.2 %copy-start = (f32[32,1280]{1,0:T(8,128)S(1)}, f32[32,1280]{1,0:T(8,128)}, u32[]{:S(2)}) copy-start(f32[32,1280]{1,0:T(8,128)} %block.1) | copy-start | bytes 491524
  1.5 1.2 %copy-start.1 = (f32[125,125]{1,0:T(8,128)S(1)}, f32[125,125]{1,0:T(8,128)}, u32[]{:S(2)}) copy-start(f32[125,125]{1,0:T(8,128)} %stiff.1) | copy-start | bytes 187504
  1.5 1.2 %copy-start.2 = (s32[9,2,256]{2,1,0:T(2,128)S(1)}, s32[9,2,256]{2,1,0:T(2,128)}, u32[]{:S(2)}) copy-start(s32[9,2,256]{2,1,0:T(2,128)} %pnodes.1) | copy-start | bytes 55300
  1.6 1.2 %copy-start.3 = (s32[8,128]{1,0:T(8,128)S(1)}, s32[8,128]{1,0:T(8,128)}, u32[]{:S(2)}) copy-start(s32[8,128]{1,0:T(8,128)} %sends.1) | copy-start | bytes 12292
  1.6 1.2 %copy-start.4 = (f32[2,18]{1,0:T(2,128)S(1)}, f32[2,18]{1,0:T(2,128)}, u32[]{:S(2)}) copy-start(f32[2,18]{1,0:T(2,128)} %coup.1) | copy-start | bytes 436
  1.6 1.2 %copy-start.5 = (f32[32]{0:T(128)S(1)}, f32[32]{0:T(128)}, u32[]{:S(2)}) copy-start(f32[32]{0:T(128)} %cscale.1) | copy-start | bytes 388

commit v2 on v1

v2 whole, which is shorter than its diff:
```python
import functools

import jax
import jax.numpy as jnp
from jax import lax
from jax.experimental import pallas as pl
from jax.experimental.pallas import tpu as pltpu
from jax.sharding import PartitionSpec as P

DEGREES = 3
CHEB_CENTER = 5.0
CHEB_HALF = 6.0
MESH = pl.DeviceIdType.MESH
OFFS = ((-1, -1), (-1, 0), (-1, 1), (0, -1), (0, 1), (1, -1), (1, 0), (1, 1))
DIAGONAL_FIRST = (0, 2, 5, 7, 1, 6, 3, 4)

VEC = 32
NODE = 1280
OWN = 5
GHO = 4
LO = 256
CN = 125
CELLS = 32
SLOTS = CELLS * 128
SENDS = 1024
PRO = 18
PPAD = 24
PK = 2 * PPAD
PALL = 9 * PK
BF = jnp.bfloat16
F32 = jnp.float32


def split(x):
    hi = x.astype(BF)
    return hi, (x - hi.astype(F32)).astype(BF)


def both(x):
    hi, lo = split(x)
    return jnp.concatenate([hi, lo], axis=0)


def dot(a, b):
    return jnp.dot(a, b, preferred_element_type=F32)


def dot_nt(a, b):
    return lax.dot_general(a, b, (((1,), (1,)), ((), ())), preferred_element_type=F32)


def block_of(got, th):
    row = th * 2 * VEC
    return got[row:row + VEC] + got[row + VEC:row + 2 * VEC]


def picked(got, high, first, count, acc):
    for th in range(count):
        one = block_of(got, th)
        acc = one if acc is None else jnp.where(high == first + th, one, acc)
    return acc


def hot_rows(row, iota):
    return jnp.where(iota == (row & (LO - 1)), 1.0, 0.0).astype(BF)


def kernel(
    nx, ny,
    block, pot, cnodes, stiff, sends, pnodes, pvals, coup, cscale,
    out,
    field, prev, own, cellown, flhs, glhs, klhs, slhs, blhs, eall,
    ct, ohg, hi8, mb, ohsend, shi8, smb, whi, wlo, kf, kmat, crow, cslab,
    sva, rva, svb, rvb, svc, rvc, sve, rve,
    sema, sema_r, semb, semb_r, semc, semc_r, seme, seme_r,
):
    ix = lax.axis_index("mx")
    iy = lax.axis_index("my")

    def at(ox, oy):
        return (lax.rem(ix + ox + nx, nx), lax.rem(iy + oy + ny, ny))

    if REMOTE:
        barrier = pltpu.get_barrier_semaphore()
        for ox, oy in OFFS:
            pl.semaphore_signal(barrier, inc=1, device_id=at(ox, oy), device_id_type=MESH)

    sub = lax.broadcasted_iota(jnp.int32, (LO, 128), 0)
    for k in range(8):
        at_k = slice(k * 128, (k + 1) * 128)
        row = sends[k:k + 1, :]
        ohsend[:, at_k] = hot_rows(row, sub)
        high = jnp.broadcast_to(row >> 8, (16, 128))
        shi8[:, at_k] = high[0:8]
        for th in range(OWN):
            smb[th, :, at_k] = jnp.where(high == th, 1.0, 0.0).astype(BF)

    ct[...] = jnp.full((CELLS, 128), -1, jnp.int32)
    ct[:, 0:CN] = cnodes[...]
    for c in range(CELLS):
        at_c = slice(c * 128, (c + 1) * 128)
        row = ct[c:c + 1, :]
        ohg[:, at_c] = hot_rows(row, sub)
        high = jnp.broadcast_to(row >> 8, (16, 128))
        hi8[:, at_c] = high[0:8]
        for th in range(OWN + GHO):
            mb[th, :, at_c] = jnp.where(high == th, 1.0, 0.0).astype(BF)

    sub2 = lax.broadcasted_iota(jnp.int32, (LO, LO), 0)
    pad = jnp.zeros((PPAD - PRO, LO), F32)
    for k in range(9):
        parts = []
        for a in range(2):
            row = pnodes[k, a:a + 1, :]
            high = jnp.broadcast_to(row >> 8, (16, LO))
            v = jnp.concatenate([pvals[k, :, a, :], pad], axis=0)
            vhi = v.astype(BF).astype(F32)
            v2 = jnp.concatenate([vhi, v - vhi], axis=0).astype(BF)
            rows = []
            for th in range(OWN):
                mask = jnp.where(high == th, 1.0, 0.0).astype(BF)
                rows.append(v2 * jnp.concatenate([mask] * 3, axis=0))
            got = dot_nt(jnp.concatenate(rows, axis=0), hot_rows(row, sub2))
            parts.append([got[th * PK:th * PK + PPAD] + got[th * PK + PPAD:(th + 1) * PK] for th in range(OWN)])
        for th in range(OWN):
            hi, lo = split(jnp.concatenate([parts[0][th], parts[1][th]], axis=0))
            whi[k * PK:(k + 1) * PK, th * LO:(th + 1) * LO] = hi
            wlo[k * PK:(k + 1) * PK, th * LO:(th + 1) * LO] = lo

    kf[...] = jnp.zeros((128, 128), F32)
    kf[0:CN, 0:CN] = stiff[...]
    khi, klo = split(kf[...])
    for r in range(2):
        kmat[r * 128:(r + 1) * 128, 0:128] = khi
        kmat[r * 128:(r + 1) * 128, 128:256] = klo

    crow[...] = jnp.zeros_like(crow)
    for h in range(2):
        for a in range(2):
            start = 64 * h + PPAD * a
            crow[0:1, start:start + PRO] = coup[a:a + 1, :]
    for m in range(DEGREES):
        for k in range(8):
            svc[m, k] = jnp.zeros((16, 128), F32)
    cslab[...] = jnp.zeros_like(cslab)

    field[...] = block[...]
    prev[...] = jnp.zeros_like(prev)

    def apply(m, carry):
        def copies(src, dst, send, recv, sign):
            return [
                pltpu.make_async_remote_copy(
                    src_ref=src.at[m, k], dst_ref=dst.at[m, k], send_sem=send.at[m, k], recv_sem=recv.at[m, k],
                    device_id=at(sign * OFFS[k][0], sign * OFFS[k][1]), device_id_type=MESH,
                )
                for k in range(8)
            ]

        ghosts = copies(sva, rva, sema, sema_r, 1)
        sums = copies(svc, rvc, semc, semc_r, 1)
        backs = copies(svb, rvb, semb, semb_r, -1)
        coefs = copies(sve, rve, seme, seme_r, -1)

        def start(group):
            if REMOTE:
                for k in DIAGONAL_FIRST:
                    group[k].start()

        def arrive(group):
            if REMOTE:
                for k in DIAGONAL_FIRST[::-1]:
                    group[k].wait_recv()

        f = field[...]
        for th in range(OWN):
            flhs[th * 2 * VEC:(th + 1) * 2 * VEC, :] = both(f[:, th * LO:(th + 1) * LO])

        for j in range(4):
            at_j = slice(j * LO, (j + 1) * LO)
            acc = picked(dot(flhs[...], ohsend[:, at_j]), shi8[0:1, at_j], 0, OWN, None)
            sva[m, 2 * j] = acc[:, 0:128]
            sva[m, 2 * j + 1] = acc[:, 128:256]

        if REMOTE:
            @pl.when(m == 0)
            def _():
                pl.semaphore_wait(barrier, 8)

        start(ghosts)

        f2 = both(f)
        c2 = dot_nt(f2, whi[...])
        c = c2[0:VEC] + c2[VEC:2 * VEC] + dot_nt(f2[0:VEC], wlo[...])
        for k in range(9):
            piece = c[:, k * PK:(k + 1) * PK]
            if k == 4:
                cslab[:, 0:PK] = piece[0:16]
                cslab[:, 64:64 + PK] = piece[16:32]
            else:
                d = k if k < 4 else k - 1
                svc[m, d, :, 0:PK] = piece[0:16]
                svc[m, d, :, 64:64 + PK] = piece[16:32]
        start(sums)

        for j in range(SLOTS // LO):
            at_j = slice(j * LO, (j + 1) * LO)
            cellown[:, at_j] = picked(dot(flhs[...], ohg[:, at_j]), hi8[0:1, at_j], 0, OWN, None)

        arrive(ghosts)
        for t in range(GHO):
            glhs[t * 2 * VEC:(t + 1) * 2 * VEC, 0:128] = both(rva[m, 2 * t])
            glhs[t * 2 * VEC:(t + 1) * 2 * VEC, 128:256] = both(rva[m, 2 * t + 1])
        for j in range(SLOTS // LO):
            at_j = slice(j * LO, (j + 1) * LO)
            high = hi8[0:1, at_j]
            acc = jnp.where(high >= 0, cellown[:, at_j], 0.0)
            acc = picked(dot(glhs[...], ohg[:, at_j]), high, OWN, GHO, acc)
            hi, lo = split(acc)
            for h in range(2):
                rows = slice((2 * j + h) * VEC, (2 * j + h + 1) * VEC)
                klhs[rows, 0:128] = hi[:, h * 128:(h + 1) * 128]
                klhs[rows, 128:256] = lo[:, h * 128:(h + 1) * 128]

        for j in range(CELLS // 8):
            got = dot(klhs[j * 256:(j + 1) * 256, :], kmat[...])
            prod = got[:, 0:128] + got[:, 128:256]
            for i in range(8):
                c0 = j * 8 + i
                at_c = slice(c0 * 128, (c0 + 1) * 128)
                pair = both(prod[i * VEC:(i + 1) * VEC] * cscale[c0])
                for th in range(OWN + GHO):
                    mask = jnp.concatenate([mb[th, :, at_c]] * 4, axis=0)
                    slhs[th * 2 * VEC:(th + 1) * 2 * VEC, at_c] = pair * mask

        arrive(sums)
        total = cslab[...]
        for k in range(8):
            total = total + (rvc if REMOTE else svc)[m, k]
        coef = total * crow[0:1, :]
        for k in range(8):
            sve[m, k] = coef
        start(coefs)

        got = dot_nt(slhs[OWN * 2 * VEC:(OWN + GHO) * 2 * VEC, :], ohg[...])
        for t in range(GHO):
            one = block_of(got, t)
            svb[m, 2 * t] = one[:, 0:128]
            svb[m, 2 * t + 1] = one[:, 128:256]
        start(backs)

        got = dot_nt(slhs[0:OWN * 2 * VEC, :], ohg[...])
        base = (pot[...] - CHEB_CENTER) * field[...]
        arrive(coefs)
        for k in range(9):
            slab = coef if k == 4 else (rve if REMOTE else sve)[m, k if k < 4 else k - 1]
            eall[0:16, k * PK:(k + 1) * PK] = slab[:, 0:PK]
            eall[16:32, k * PK:(k + 1) * PK] = slab[:, 64:64 + PK]
        e2 = both(eall[...])
        s2 = dot(e2, whi[...])
        base = base + (s2[0:VEC] + s2[VEC:2 * VEC] + dot(e2[0:VEC], wlo[...]))
        for th in range(OWN):
            at_t = slice(th * LO, (th + 1) * LO)
            own[:, at_t] = block_of(got, th) + base[:, at_t]

        arrive(backs)
        for k in range(8):
            at_k = slice(k * 128, (k + 1) * 128)
            pair = both((rvb if REMOTE else svb)[m, k])
            for th in range(OWN):
                blhs[th * 2 * VEC:(th + 1) * 2 * VEC, at_k] = pair * jnp.concatenate([smb[th, :, at_k]] * 4, axis=0)
        got = dot_nt(blhs[...], ohsend[...])
        alpha = jnp.where(m == 0, 1.0 / CHEB_HALF, 2.0 / CHEB_HALF)
        for th in range(OWN):
            at_t = slice(th * LO, (th + 1) * LO)
            new = alpha * (own[:, at_t] + block_of(got, th)) - prev[:, at_t]
            prev[:, at_t] = field[:, at_t]
            field[:, at_t] = new
        if REMOTE:
            for group in (ghosts, sums, backs, coefs):
                for one in group:
                    one.wait_send()
        return carry

    lax.fori_loop(0, DEGREES, apply, 0)
    out[...] = field[...]


REMOTE = True


def shards(block, potential, cell_nodes, cell_scale, stiffness, send_nodes, proj_nodes, proj_values, coupling):
    nx, ny = lax.axis_size("mx"), lax.axis_size("my")
    vmem = pl.BlockSpec(memory_space=pltpu.VMEM)
    smem = pl.BlockSpec(memory_space=pltpu.SMEM)
    halo = pltpu.VMEM((DEGREES, 8, VEC, 128), F32)
    slab = pltpu.VMEM((DEGREES, 8, 16, 128), F32)
    sem = pltpu.SemaphoreType.DMA((DEGREES, 8))
    return pl.pallas_call(
        functools.partial(kernel, nx, ny),
        out_shape=jax.ShapeDtypeStruct((VEC, NODE), F32),
        in_specs=[vmem] * 8 + [smem],
        out_specs=vmem,
        scratch_shapes=[
            pltpu.VMEM((VEC, NODE), F32),
            pltpu.VMEM((VEC, NODE), F32),
            pltpu.VMEM((VEC, NODE), F32),
            pltpu.VMEM((VEC, SLOTS), F32),
            pltpu.VMEM((OWN * 2 * VEC, LO), BF),
            pltpu.VMEM((GHO * 2 * VEC, LO), BF),
            pltpu.VMEM((CELLS * VEC, 256), BF),
            pltpu.VMEM(((OWN + GHO) * 2 * VEC, SLOTS), BF),
            pltpu.VMEM((OWN * 2 * VEC, SENDS), BF),
            pltpu.VMEM((VEC, PALL), F32),
            pltpu.VMEM((CELLS, 128), jnp.int32),
            pltpu.VMEM((LO, SLOTS), BF),
            pltpu.VMEM((8, SLOTS), jnp.int32),
            pltpu.VMEM((OWN + GHO, 16, SLOTS), BF),
            pltpu.VMEM((LO, SENDS), BF),
            pltpu.VMEM((8, SENDS), jnp.int32),
            pltpu.VMEM((OWN, 16, SENDS), BF),
            pltpu.VMEM((PALL, NODE), BF),
            pltpu.VMEM((PALL, NODE), BF),
            pltpu.VMEM((128, 128), F32),
            pltpu.VMEM((256, 256), BF),
            pltpu.VMEM((8, 128), F32),
            pltpu.VMEM((16, 128), F32),
            halo, halo, halo, halo, slab, slab, slab, slab,
            sem, sem, sem, sem, sem, sem, sem, sem,
        ],
        compiler_params=pltpu.CompilerParams(
            collective_id=0, has_side_effects=True, vmem_limit_bytes=48 * 1024 * 1024
        ) if REMOTE else pltpu.CompilerParams(has_side_effects=True, vmem_limit_bytes=48 * 1024 * 1024),
        name="filtered",
    )(
        block, potential.reshape(1, NODE), cell_nodes.T, stiffness, send_nodes, proj_nodes,
        proj_values.transpose(0, 2, 1, 3), coupling, cell_scale,
    )


def solution(mesh):
    axes = ("mx", "my")
    placed = (
        P(None, axes), P(axes), P(None, axes), P(axes), P(), P(None, axes),
        P(None, axes, None), P(None, axes, None, None), P(axes, None),
    )
    return jax.shard_map(shards, mesh=mesh, in_specs=placed, out_specs=P(None, axes), check_vma=False)
```

time: 85.2 us -> 65.5 us (0.77)
  Pallas kernels: 81.5 us -> 58.8 us
  local copies, waits for them, and re-layouts: 3.35 us -> 6.21 us
    pallas_call x1, Pallas kernels: 81.5 us -> 58.8 us  [shards(): pl.pallas_call(functools.partial(kernel, nx, ny), out_shape=jax.ShapeDtyp...]
    unnamed x15 -> x17, local copies, waits for them, and re-layouts: 2.65 us -> 5.49 us
where the time goes in v2:
time: 65.5 us; the launch traced here: 65.1 us
  Pallas kernels  58.8 us (90%)
  local copies, waits for them, and re-layouts  6.21 us (9%)
    pallas_call x1, Pallas kernels, shards(): pl.pallas_call(functools.partial(kernel, nx, ny), out_shape=jax.ShapeDtyp...  58.8 us
    unnamed x17, local copies, waits for them, and re-layouts  5.49 us

profile of v2, /device:TPU:1, one launch (start us, length us, event | category | flops | bytes accessed | tf_op | source)
XLA Modules:
  0.0 65.1 jit_solution(12306895358838180700)
XLA Ops:
  0.0 0.0 copy-start.4
  0.0 0.0 copy-start.7
  0.0 0.7 %reshape.3.pot = f32[1,1280]{1,0:T(1,128)S(1)} reshape(f32[1280]{0:T(1024)} %param.10) | data formatting | bytes 10240 | tf_op jit(solution)/shard_map/reshape | solution.py:336
  0.7 0.0 copy-done.4
  0.7 0.0 copy-done.7
  0.7 0.0 copy-start
  0.8 1.0 %copy-done = f32[9,2,18,256]{3,1,2,0:T(2,128)S(1)} copy-done((f32[9,2,18,256]{3,1,2,0:T(2,128)S(1)}, f32[9,2,18,256]{3,1,2,0:T(2,128)}, u32[]{:S(2)}) %copy-start) | copy-done | bytes 331800
  1.7 0.0 copy-start.1
  1.7 0.9 %copy-done.1 = f32[32,1280]{1,0:T(8,128)S(1)} copy-done((f32[32,1280]{1,0:T(8,128)S(1)}, f32[32,1280]{1,0:T(8,128)}, u32[]{:S(2)}) %copy-start.1) | copy-done | bytes 163864
  2.6 0.0 copy-start.2
  2.6 0.8 %copy-done.2 = f32[125,125]{1,0:T(8,128)S(1)} copy-done((f32[125,125]{1,0:T(8,128)S(1)}, f32[125,125]{1,0:T(8,128)}, u32[]{:S(2)}) %copy-start.2) | copy-done | bytes 62524
  3.5 0.0 copy-start.3
  3.5 0.7 %copy-done.3 = s32[9,2,256]{2,1,0:T(2,128)S(1)} copy-done((s32[9,2,256]{2,1,0:T(2,128)S(1)}, s32[9,2,256]{2,1,0:T(2,128)}, u32[]{:S(2)}) %copy-start.3) | copy-done | bytes 18456
  4.2 0.0 copy-start.5
  4.2 0.7 %copy-done.5 = s32[8,128]{1,0:T(8,128)S(1)} copy-done((s32[8,128]{1,0:T(8,128)S(1)}, s32[8,128]{1,0:T(8,128)}, u32[]{:S(2)}) %copy-start.5) | copy-done | bytes 4120
  4.9 0.0 copy-start.6
  4.9 0.7 %copy-done.6 = f32[2,18]{1,0:T(2,128)S(1)} copy-done((f32[2,18]{1,0:T(2,128)S(1)}, f32[2,18]{1,0:T(2,128)}, u32[]{:S(2)}) %copy-start.6) | copy-done | bytes 168
  5.6 58.8 %filtered.1 = f32[32,1280]{1,0:T(8,128)S(1)} custom-call(f32[32,1280]{1,0:T(8,128)S(1)} %copy-done.1, f32[1,1280]{1,0:T(1,128)S(1)} %reshape.3.pot, s32[32,125]{1,0:T(8,128)S(1)} %bitcast.3, f32[125,125]{1,0:T(8,128)S(1)} %copy-done.2, s32[8,128]{1,0:T(8,128)S(1)} %copy-done.5, s32[9,2,256]{2,1,0:T(2,128)S(1)} %copy-done.3, f32[9,18,2,256]{3,2,1,0:T(2,128)S(1)} %bitcast.2, ...), custom_call_target="tpu_custom_call" | custom-call | tf_op jit(solution)/shard_map/filtered/pallas_call | solution.py:299
  64.4 0.7 %copy.11 = f32[32,1280]{1,0:T(8,128)} copy(f32[32,1280]{1,0:T(8,128)S(1)} %filtered.1) | data formatting | bytes 327680
Async XLA Ops:
  0.0 0.7 %copy-start.4 = (s32[125,32]{0,1:T(8,128)S(1)}, s32[125,32]{0,1:T(8,128)}, u32[]{:S(2)}) copy-start(s32[125,32]{0,1:T(8,128)} %param.11) | copy-start | bytes 48004
  0.0 0.7 %copy-start.7 = (f32[32]{0:T(128)S(1)}, f32[32]{0:T(128)}, u32[]{:S(2)}) copy-start(f32[32]{0:T(128)} %cscale.1) | copy-start | bytes 388
  0.7 1.0 %copy-start = (f32[9,2,18,256]{3,1,2,0:T(2,128)S(1)}, f32[9,2,18,256]{3,1,2,0:T(2,128)}, u32[]{:S(2)}) copy-start(f32[9,2,18,256]{3,1,2,0:T(2,128)} %param.16) | copy-start | bytes 995332
  1.7 0.9 %copy-start.1 = (f32[32,1280]{1,0:T(8,128)S(1)}, f32[32,1280]{1,0:T(8,128)}, u32[]{:S(2)}) copy-start(f32[32,1280]{1,0:T(8,128)} %block.1) | copy-start | bytes 491524
  2.6 0.8 %copy-start.2 = (f32[125,125]{1,0:T(8,128)S(1)}, f32[125,125]{1,0:T(8,128)}, u32[]{:S(2)}) copy-start(f32[125,125]{1,0:T(8,128)} %stiff.1) | copy-start | bytes 187504
  3.5 0.7 %copy-start.3 = (s32[9,2,256]{2,1,0:T(2,128)S(1)}, s32[9,2,256]{2,1,0:T(2,128)}, u32[]{:S(2)}) copy-start(s32[9,2,256]{2,1,0:T(2,128)} %pnodes.1) | copy-start | bytes 55300
  4.2 0.7 %copy-start.5 = (s32[8,128]{1,0:T(8,128)S(1)}, s32[8,128]{1,0:T(8,128)}, u32[]{:S(2)}) copy-start(s32[8,128]{1,0:T(8,128)} %sends.1) | copy-start | bytes 12292
  4.9 0.7 %copy-start.6 = (f32[2,18]{1,0:T(2,128)S(1)}, f32[2,18]{1,0:T(2,128)}, u32[]{:S(2)}) copy-start(f32[2,18]{1,0:T(2,128)} %coup.1) | copy-start | bytes 436

commit v3 on v2

v3 whole, which is shorter than its diff:
```python
import functools

import jax
import jax.numpy as jnp
from jax import lax
from jax.experimental import pallas as pl
from jax.experimental.pallas import tpu as pltpu
from jax.sharding import PartitionSpec as P

DEGREES = 3
CHEB_CENTER = 5.0
CHEB_HALF = 6.0
MESH = pl.DeviceIdType.MESH
OFFS = ((-1, -1), (-1, 0), (-1, 1), (0, -1), (0, 1), (1, -1), (1, 0), (1, 1))
CARD, DIAG = (1, 6, 3, 4), (0, 2, 5, 7)
ORDER = CARD + DIAG

VEC = 32
NODE = 1280
OWN = 5
GHO = 4
LO = 256
CN = 125
CELLS = 32
SLOTS = CELLS * 128
SENDS = 1024
PRO = 18
PPAD = 24
PK = 2 * PPAD
PALL = 9 * PK
BF = jnp.bfloat16
F32 = jnp.float32


def split(x):
    hi = x.astype(BF)
    return hi, (x - hi.astype(F32)).astype(BF)


def both(x):
    hi, lo = split(x)
    return jnp.concatenate([hi, lo], axis=0)


def dot(a, b):
    return jnp.dot(a, b, preferred_element_type=F32)


def dot_nt(a, b):
    return lax.dot_general(a, b, (((1,), (1,)), ((), ())), preferred_element_type=F32)


def block_of(got, th):
    row = th * 2 * VEC
    return got[row:row + VEC] + got[row + VEC:row + 2 * VEC]


def picked(got, high, first, count, acc):
    for th in range(count):
        one = block_of(got, th)
        acc = one if acc is None else jnp.where(high == first + th, one, acc)
    return acc


def hot_rows(row, iota):
    return jnp.where(iota == (row & (LO - 1)), 1.0, 0.0).astype(BF)


def kernel(
    nx, ny,
    a_block, a_pot, a_cnodes, a_stiff, a_sends, a_pnodes, a_pvals, a_coup, a_cscale,
    out,
    block, pot, cnodes, stiff, sends, pnodes, pvals, coup, cscale, insem,
    prev, own, cellown, flhs, glhs, klhs, prods, slhs, blhs, eall,
    ct, ohg, hi8, mb, ohs, ohsend, shi8, smb, ohb, wf, whi, wlo, twhi, twlo, kf, kmat, crow, cslab,
    sva, rva, svb, rvb, svc, rvc, sve, rve,
    sema, sema_r, semb, semb_r, semc, semc_r, seme, seme_r,
):
    ix = lax.axis_index("mx")
    iy = lax.axis_index("my")

    def at(ox, oy):
        return (lax.rem(ix + ox + nx, nx), lax.rem(iy + oy + ny, ny))

    if REMOTE:
        barrier = pltpu.get_barrier_semaphore()
        for k in ORDER[::-1]:
            pl.semaphore_signal(barrier, inc=1, device_id=at(*OFFS[k]), device_id_type=MESH)

    pairs = (
        (a_sends, sends), (a_block, block), (a_cnodes, cnodes), (a_pnodes, pnodes), (a_pvals, pvals),
        (a_stiff, stiff), (a_coup, coup), (a_cscale, cscale), (a_pot, pot),
    )
    loads = {id(dst): pltpu.make_async_copy(src, dst, insem.at[i]) for i, (src, dst) in enumerate(pairs)}
    for one in loads.values():
        one.start()

    def ready(*refs):
        for ref in refs:
            loads[id(ref)].wait()

    def copies(m, src, dst, send, recv, sign):
        return {
            k: pltpu.make_async_remote_copy(
                src_ref=src.at[m, k], dst_ref=dst.at[m, k], send_sem=send.at[m, k], recv_sem=recv.at[m, k],
                device_id=at(sign * OFFS[k][0], sign * OFFS[k][1]), device_id_type=MESH,
            )
            for k in range(8)
        } if REMOTE else {}

    def start(group, which):
        for k in which:
            if REMOTE:
                group[k].start()

    def arrive(group, which):
        for k in which:
            if REMOTE:
                group[k].wait_recv()

    def sent(*groups):
        for group in groups:
            for one in group.values():
                one.wait_send()

    def send_values(m, before_first):
        ghosts = copies(m, sva, rva, sema, sema_r, 1)
        for j in (2, 3, 0, 1):
            at_j = slice(j * LO, (j + 1) * LO)
            acc = picked(dot(flhs[...], ohsend[:, at_j]), shi8[0:1, at_j], 0, OWN, None)
            sva[m, ORDER[2 * j]] = acc[:, 0:128]
            sva[m, ORDER[2 * j + 1]] = acc[:, 128:256]
            if j == 3:
                before_first()
                start(ghosts, DIAG)
        start(ghosts, CARD)

    def field_rows():
        for th in range(OWN):
            flhs[th * 2 * VEC:(th + 1) * 2 * VEC, :] = both(out[:, th * LO:(th + 1) * LO])

    sub = lax.broadcasted_iota(jnp.int32, (LO, 128), 0)
    ready(sends)
    for q, k in enumerate(ORDER):
        at_q = slice(q * 128, (q + 1) * 128)
        row = sends[k:k + 1, :]
        ohsend[:, at_q] = hot_rows(row, sub)
        shi8[:, at_q] = jnp.broadcast_to(row >> 8, (8, 128))
    ready(block)
    out[...] = block[...]
    field_rows()

    def met():
        if REMOTE:
            pl.semaphore_wait(barrier, 8)

    send_values(0, met)

    ct[...] = jnp.full((128, 128), -1, jnp.int32)
    ready(cnodes)
    ct[0:CELLS, 0:CN] = cnodes[...]
    pos = ct[0:CELLS, :]
    slot = (pos >> 7) - 2 * OWN
    new = slot
    for q, k in enumerate(ORDER):
        new = jnp.where(slot == k, q, new)
    ct[0:CELLS, :] = jnp.where(slot >= 0, ((new + 2 * OWN) << 7) + (pos & 127), pos)
    for q, k in enumerate(ORDER):
        ct[CELLS + q:CELLS + q + 1, :] = sends[k:k + 1, :]
    cols = ct[...].T
    lane = lax.broadcasted_iota(jnp.int32, (128, LO), 1)
    for c in range(CELLS):
        at_c = slice(c * 128, (c + 1) * 128)
        row = ct[c:c + 1, :]
        ohg[:, at_c] = hot_rows(row, sub)
        ohs[at_c, :] = hot_rows(jnp.broadcast_to(cols[:, c:c + 1], (128, LO)), lane)
        high = jnp.broadcast_to(row >> 8, (16, 128))
        hi8[:, at_c] = high[0:8]
        for th in range(OWN + GHO):
            mb[th, :, at_c] = jnp.where(high == th, 1.0, 0.0).astype(BF)
    for q in range(8):
        at_q = slice(q * 128, (q + 1) * 128)
        high = jnp.broadcast_to(ct[CELLS + q:CELLS + q + 1, :] >> 8, (16, 128))
        ohb[at_q, :] = hot_rows(jnp.broadcast_to(cols[:, CELLS + q:CELLS + q + 1], (128, LO)), lane)
        for th in range(OWN):
            smb[th, :, at_q] = jnp.where(high == th, 1.0, 0.0).astype(BF)

    ready(pnodes, pvals)
    sub2 = lax.broadcasted_iota(jnp.int32, (LO, LO), 0)
    pad = jnp.zeros((PPAD - PRO, LO), F32)
    for k in range(9):
        parts = []
        for a in range(2):
            row = pnodes[k, a:a + 1, :]
            high = jnp.broadcast_to(row >> 8, (16, LO))
            v = jnp.concatenate([pvals[k, :, a, :], pad], axis=0)
            vhi = v.astype(BF).astype(F32)
            v2 = jnp.concatenate([vhi, v - vhi], axis=0).astype(BF)
            rows = []
            for th in range(OWN):
                mask = jnp.where(high == th, 1.0, 0.0).astype(BF)
                rows.append(v2 * jnp.concatenate([mask] * 3, axis=0))
            got = dot_nt(jnp.concatenate(rows, axis=0), hot_rows(row, sub2))
            parts.append([got[th * PK:th * PK + PPAD] + got[th * PK + PPAD:(th + 1) * PK] for th in range(OWN)])
        for th in range(OWN):
            at_t = slice(th * LO, (th + 1) * LO)
            w = jnp.concatenate([parts[0][th], parts[1][th]], axis=0)
            hi, lo = split(w)
            wf[k * PK:(k + 1) * PK, at_t] = w
            whi[k * PK:(k + 1) * PK, at_t] = hi
            wlo[k * PK:(k + 1) * PK, at_t] = lo
    wf[PALL:512, :] = jnp.zeros((512 - PALL, NODE), F32)
    for n in range(NODE // 128):
        at_n = slice(n * 128, (n + 1) * 128)
        for r in range(4):
            at_r = slice(r * 128, (r + 1) * 128)
            hi, lo = split(wf[at_r, at_n].T)
            twhi[at_n, at_r] = hi
            twlo[at_n, at_r] = lo

    ready(stiff, coup, cscale, pot)
    kf[...] = jnp.zeros((128, 128), F32)
    kf[0:CN, 0:CN] = stiff[...]
    khi, klo = split(kf[...])
    for r in range(2):
        kmat[r * 128:(r + 1) * 128, 0:128] = khi
        kmat[r * 128:(r + 1) * 128, 128:256] = klo

    crow[...] = jnp.zeros_like(crow)
    for h in range(2):
        for a in range(2):
            first = 64 * h + PPAD * a
            crow[0:1, first:first + PRO] = coup[a:a + 1, :]
    for m in range(DEGREES):
        for k in range(8):
            svc[m, k] = jnp.zeros((16, 128), F32)
    cslab[...] = jnp.zeros_like(cslab)
    prev[...] = jnp.zeros_like(prev)

    def masked(th, at_c):
        return prods[:, at_c] * jnp.concatenate([mb[th, :, at_c]] * 4, axis=0)

    def scatter_rows(first, count):
        for th in range(first, first + count):
            for c in range(SLOTS // 512):
                at_c = slice(c * 512, (c + 1) * 512)
                slhs[th * 2 * VEC:(th + 1) * 2 * VEC, at_c] = masked(th, at_c)
        return dot(slhs[first * 2 * VEC:(first + count) * 2 * VEC, :], ohs[...])

    def apply(m, carry):
        ghosts = copies(m, sva, rva, sema, sema_r, 1)
        sums = copies(m, svc, rvc, semc, semc_r, 1)
        backs = copies(m, svb, rvb, semb, semb_r, -1)
        coefs = copies(m, sve, rve, seme, seme_r, -1)

        f2 = both(out[...])
        c2 = dot(f2, twhi[...])
        c = c2[0:VEC] + c2[VEC:2 * VEC] + dot(f2[0:VEC], twlo[...])
        for k in range(9):
            piece = c[:, k * PK:(k + 1) * PK]
            if k == 4:
                cslab[:, 0:PK] = piece[0:16]
                cslab[:, 64:64 + PK] = piece[16:32]
            else:
                d = k if k < 4 else k - 1
                svc[m, d, :, 0:PK] = piece[0:16]
                svc[m, d, :, 64:64 + PK] = piece[16:32]
        start(sums, ORDER[::-1])

        for j in range(SLOTS // LO):
            at_j = slice(j * LO, (j + 1) * LO)
            acc = picked(dot(flhs[...], ohg[:, at_j]), hi8[0:1, at_j], 0, OWN, None)
            cellown[:, at_j] = jnp.where(hi8[0:1, at_j] >= 0, acc, 0.0)

        def ghost_columns(first, which, use):
            arrive(ghosts, which)
            for t in range(first, first + 2):
                glhs[t * 2 * VEC:(t + 1) * 2 * VEC, 0:128] = both((rva if REMOTE else sva)[m, ORDER[2 * t]])
                glhs[t * 2 * VEC:(t + 1) * 2 * VEC, 128:256] = both((rva if REMOTE else sva)[m, ORDER[2 * t + 1]])
            part = glhs[first * 2 * VEC:(first + 2) * 2 * VEC, :]
            for j in range(SLOTS // LO):
                at_j = slice(j * LO, (j + 1) * LO)
                use(j, at_j, picked(dot(part, ohg[:, at_j]), hi8[0:1, at_j], OWN + first, 2, cellown[:, at_j]))

        def keep(j, at_j, acc):
            cellown[:, at_j] = acc

        def stack(j, at_j, acc):
            hi, lo = split(acc)
            for h in range(2):
                rows = slice((2 * j + h) * VEC, (2 * j + h + 1) * VEC)
                klhs[rows, 0:128] = hi[:, h * 128:(h + 1) * 128]
                klhs[rows, 128:256] = lo[:, h * 128:(h + 1) * 128]

        ghost_columns(0, CARD, keep)
        ghost_columns(2, DIAG, stack)

        for j in range(CELLS // 8):
            got = dot(klhs[j * 256:(j + 1) * 256, :], kmat[...])
            prod = got[:, 0:128] + got[:, 128:256]
            for i in range(8):
                c0 = j * 8 + i
                prods[:, c0 * 128:(c0 + 1) * 128] = both(prod[i * VEC:(i + 1) * VEC] * cscale[c0])

        arrive(sums, ORDER)
        total = cslab[...]
        for k in range(8):
            total = total + (rvc if REMOTE else svc)[m, k]
        coef = total * crow[0:1, :]
        for k in range(8):
            sve[m, k] = coef
        start(coefs, ORDER[::-1])

        def give_back(first, which):
            got = scatter_rows(OWN + first, 2)
            for t in range(2):
                one = block_of(got, t)
                svb[m, ORDER[2 * (first + t)]] = one[:, 0:128]
                svb[m, ORDER[2 * (first + t) + 1]] = one[:, 128:256]
            start(backs, which)

        give_back(2, DIAG)
        give_back(0, CARD)

        got = scatter_rows(0, OWN)
        for n in range(NODE // 128):
            at_n = slice(n * 128, (n + 1) * 128)
            own[:, at_n] = (pot[n:n + 1, :] - CHEB_CENTER) * out[:, at_n]
        for th in range(OWN):
            own[:, th * LO:(th + 1) * LO] += block_of(got, th)
        sent(ghosts, sums)
        arrive(coefs, ORDER)
        for k in range(9):
            slab = coef if k == 4 else (rve if REMOTE else sve)[m, k if k < 4 else k - 1]
            eall[0:16, k * PK:(k + 1) * PK] = slab[:, 0:PK]
            eall[16:32, k * PK:(k + 1) * PK] = slab[:, 64:64 + PK]
        e2 = both(eall[...])
        s2 = dot(e2, whi[...])
        own[...] += s2[0:VEC] + s2[VEC:2 * VEC] + dot(e2[0:VEC], wlo[...])

        def take_back(first, which):
            arrive(backs, which)
            for q in range(first, first + 4):
                at_q = slice(q * 128, (q + 1) * 128)
                pair = both((rvb if REMOTE else svb)[m, ORDER[q]])
                for th in range(OWN):
                    blhs[th * 2 * VEC:(th + 1) * 2 * VEC, at_q] = pair * jnp.concatenate([smb[th, :, at_q]] * 4, axis=0)
            at_f = slice(first * 128, (first + 4) * 128)
            return dot(blhs[:, at_f], ohb[at_f, :])

        got = take_back(0, CARD)
        for th in range(OWN):
            own[:, th * LO:(th + 1) * LO] += block_of(got, th)
        got = take_back(4, DIAG)
        alpha = jnp.where(m == 0, 1.0 / CHEB_HALF, 2.0 / CHEB_HALF)
        for th in range(OWN):
            at_t = slice(th * LO, (th + 1) * LO)
            new = alpha * (own[:, at_t] + block_of(got, th)) - prev[:, at_t]
            prev[:, at_t] = out[:, at_t]
            out[:, at_t] = new

        @pl.when(m < DEGREES - 1)
        def _():
            field_rows()
            send_values(m + 1, lambda: None)

        sent(backs, coefs)
        return carry

    lax.fori_loop(0, DEGREES, apply, 0)


REMOTE = True


def shards(block, potential, cell_nodes, cell_scale, stiffness, send_nodes, proj_nodes, proj_values, coupling):
    nx, ny = lax.axis_size("mx"), lax.axis_size("my")
    vmem = pl.BlockSpec(memory_space=pltpu.VMEM)
    halo = pltpu.VMEM((DEGREES, 8, VEC, 128), F32)
    slab = pltpu.VMEM((DEGREES, 8, 16, 128), F32)
    sem = pltpu.SemaphoreType.DMA((DEGREES, 8))
    hbm = pl.BlockSpec(memory_space=pltpu.HBM)
    args = (
        block, potential.reshape(NODE // 128, 128), cell_nodes.T, stiffness, send_nodes, proj_nodes,
        proj_values.transpose(0, 2, 1, 3), coupling, cell_scale,
    )
    return pl.pallas_call(
        functools.partial(kernel, nx, ny),
        out_shape=jax.ShapeDtypeStruct((VEC, NODE), F32),
        in_specs=[hbm] * len(args),
        out_specs=vmem,
        scratch_shapes=[pltpu.VMEM(one.shape, one.dtype) for one in args[:-1]] + [
            pltpu.SMEM(cell_scale.shape, F32),
            pltpu.SemaphoreType.DMA((len(args),)),
            pltpu.VMEM((VEC, NODE), F32),
            pltpu.VMEM((VEC, NODE), F32),
            pltpu.VMEM((VEC, SLOTS), F32),
            pltpu.VMEM((OWN * 2 * VEC, LO), BF),
            pltpu.VMEM((GHO * 2 * VEC, LO), BF),
            pltpu.VMEM((CELLS * VEC, 256), BF),
            pltpu.VMEM((2 * VEC, SLOTS), BF),
            pltpu.VMEM(((OWN + GHO) * 2 * VEC, SLOTS), BF),
            pltpu.VMEM((OWN * 2 * VEC, SENDS), BF),
            pltpu.VMEM((VEC, PALL), F32),
            pltpu.VMEM((128, 128), jnp.int32),
            pltpu.VMEM((LO, SLOTS), BF),
            pltpu.VMEM((8, SLOTS), jnp.int32),
            pltpu.VMEM((OWN + GHO, 16, SLOTS), BF),
            pltpu.VMEM((SLOTS, LO), BF),
            pltpu.VMEM((LO, SENDS), BF),
            pltpu.VMEM((8, SENDS), jnp.int32),
            pltpu.VMEM((OWN, 16, SENDS), BF),
            pltpu.VMEM((SENDS, LO), BF),
            pltpu.VMEM((512, NODE), F32),
            pltpu.VMEM((PALL, NODE), BF),
            pltpu.VMEM((PALL, NODE), BF),
            pltpu.VMEM((NODE, 512), BF),
            pltpu.VMEM((NODE, 512), BF),
            pltpu.VMEM((128, 128), F32),
            pltpu.VMEM((256, 256), BF),
            pltpu.VMEM((8, 128), F32),
            pltpu.VMEM((16, 128), F32),
            halo, halo, halo, halo, slab, slab, slab, slab,
            sem, sem, sem, sem, sem, sem, sem, sem,
        ],
        compiler_params=pltpu.CompilerParams(
            collective_id=0, has_side_effects=True, vmem_limit_bytes=48 * 1024 * 1024
        ) if REMOTE else pltpu.CompilerParams(has_side_effects=True, vmem_limit_bytes=48 * 1024 * 1024),
        name="filtered",
    )(*args)


def solution(mesh):
    axes = ("mx", "my")
    placed = (
        P(None, axes), P(axes), P(None, axes), P(axes), P(), P(None, axes),
        P(None, axes, None), P(None, axes, None, None), P(axes, None),
    )
    return jax.shard_map(shards, mesh=mesh, in_specs=placed, out_specs=P(None, axes), check_vma=False)
```

time: 65.5 us -> 61.7 us (0.942)
  Pallas kernels: 58.8 us -> 55 us
    pallas_call x1, Pallas kernels: 58.8 us -> 55 us  [shards(): pl.pallas_call(functools.partial(kernel, nx, ny), out_shape=jax.ShapeDtyp...]
    unnamed x17 -> x19, local copies, waits for them, and re-layouts: 5.49 us -> 6.22 us
    reshape x1 -> x0, local copies, waits for them, and re-layouts: 0.73 us -> none  [shards(): potential.reshape(1, NODE)]
where the time goes in v3:
time: 61.7 us; the launch traced here: 61.2 us
  Pallas kernels  55 us (89%)
  local copies, waits for them, and re-layouts  6.22 us (10%)
    pallas_call x1, Pallas kernels, shards(): pl.pallas_call(functools.partial(kernel, nx, ny), out_shape=jax.ShapeDtyp...  55 us
    unnamed x19, local copies, waits for them, and re-layouts  6.22 us

profile of v3, /device:TPU:1, one launch (start us, length us, event | category | flops | bytes accessed | tf_op | source)
XLA Modules:
  0.0 61.2 jit_solution(4183223686221730603)
XLA Ops:
  0.0 0.0 copy-start.6
  0.0 0.0 copy-start.7
  0.0 0.0 copy-start.8
  0.0 0.7 %copy-done.6 = s32[8,128]{1,0:T(8,128)S(1)} copy-done((s32[8,128]{1,0:T(8,128)S(1)}, s32[8,128]{1,0:T(8,128)}, u32[]{:S(2)}) %copy-start.6) | copy-done | bytes 4120
  0.7 0.0 copy-done.7
  0.7 0.0 copy-done.8
  0.7 0.0 copy-start
  0.7 1.0 %copy-done = f32[9,2,18,256]{3,1,2,0:T(2,128)S(1)} copy-done((f32[9,2,18,256]{3,1,2,0:T(2,128)S(1)}, f32[9,2,18,256]{3,1,2,0:T(2,128)}, u32[]{:S(2)}) %copy-start) | copy-done | bytes 331800
  1.7 0.0 copy-start.1
  1.7 0.9 %copy-done.1 = f32[32,1280]{1,0:T(8,128)S(1)} copy-done((f32[32,1280]{1,0:T(8,128)S(1)}, f32[32,1280]{1,0:T(8,128)}, u32[]{:S(2)}) %copy-start.1) | copy-done | bytes 163864
  2.6 0.0 copy-start.2
  2.6 0.8 %copy-done.2 = f32[125,125]{1,0:T(8,128)S(1)} copy-done((f32[125,125]{1,0:T(8,128)S(1)}, f32[125,125]{1,0:T(8,128)}, u32[]{:S(2)}) %copy-start.2) | copy-done | bytes 62524
  3.4 0.0 copy-start.3
  3.4 0.7 %copy-done.3 = s32[9,2,256]{2,1,0:T(2,128)S(1)} copy-done((s32[9,2,256]{2,1,0:T(2,128)S(1)}, s32[9,2,256]{2,1,0:T(2,128)}, u32[]{:S(2)}) %copy-start.3) | copy-done | bytes 18456
  4.2 0.0 copy-start.4
  4.2 0.7 %copy-done.4 = s32[125,32]{0,1:T(8,128)S(1)} copy-done((s32[125,32]{0,1:T(8,128)S(1)}, s32[125,32]{0,1:T(8,128)}, u32[]{:S(2)}) %copy-start.4) | copy-done | bytes 16024
  4.9 0.0 copy-start.5
  4.9 0.7 %copy-done.5 = f32[1280]{0:T(1024)S(1)} copy-done((f32[1280]{0:T(1024)S(1)}, f32[1280]{0:T(1024)}, u32[]{:S(2)}) %copy-start.5) | copy-done | bytes 5144
  5.6 55.0 %filtered.1 = f32[32,1280]{1,0:T(8,128)S(1)} custom-call(f32[32,1280]{1,0:T(8,128)S(1)} %copy-done.1, f32[10,128]{1,0:T(8,128)S(1)} %bitcast.5, s32[32,125]{1,0:T(8,128)S(1)} %bitcast.4, f32[125,125]{1,0:T(8,128)S(1)} %copy-done.2, s32[8,128]{1,0:T(8,128)S(1)} %copy-done.6, s32[9,2,256]{2,1,0:T(2,128)S(1)} %copy-done.3, f32[9,18,2,256]{3,2,1,0:T(2,128)S(1)} %bitcast.3, ...), custom_call_target="tpu_custom_call" | custom-call | tf_op jit(solution)/shard_map/filtered/pallas_call | solution.py:387
  60.6 0.7 %copy.11 = f32[32,1280]{1,0:T(8,128)} copy(f32[32,1280]{1,0:T(8,128)S(1)} %filtered.1) | data formatting | bytes 327680
Async XLA Ops:
  0.0 0.7 %copy-start.6 = (s32[8,128]{1,0:T(8,128)S(1)}, s32[8,128]{1,0:T(8,128)}, u32[]{:S(2)}) copy-start(s32[8,128]{1,0:T(8,128)} %a_sends.1) | copy-start | bytes 12292
  0.0 0.7 %copy-start.7 = (f32[2,18]{1,0:T(2,128)S(1)}, f32[2,18]{1,0:T(2,128)}, u32[]{:S(2)}) copy-start(f32[2,18]{1,0:T(2,128)} %a_coup.1) | copy-start | bytes 436
  0.0 0.7 %copy-start.8 = (f32[32]{0:T(128)S(1)}, f32[32]{0:T(128)}, u32[]{:S(2)}) copy-start(f32[32]{0:T(128)} %a_cscale.1) | copy-start | bytes 388
  0.7 1.0 %copy-start = (f32[9,2,18,256]{3,1,2,0:T(2,128)S(1)}, f32[9,2,18,256]{3,1,2,0:T(2,128)}, u32[]{:S(2)}) copy-start(f32[9,2,18,256]{3,1,2,0:T(2,128)} %param.16) | copy-start | bytes 995332
  1.7 0.9 %copy-start.1 = (f32[32,1280]{1,0:T(8,128)S(1)}, f32[32,1280]{1,0:T(8,128)}, u32[]{:S(2)}) copy-start(f32[32,1280]{1,0:T(8,128)} %a_block.1) | copy-start | bytes 491524
  2.6 0.8 %copy-start.2 = (f32[125,125]{1,0:T(8,128)S(1)}, f32[125,125]{1,0:T(8,128)}, u32[]{:S(2)}) copy-start(f32[125,125]{1,0:T(8,128)} %a_stiff.1) | copy-start | bytes 187504
  3.4 0.7 %copy-start.3 = (s32[9,2,256]{2,1,0:T(2,128)S(1)}, s32[9,2,256]{2,1,0:T(2,128)}, u32[]{:S(2)}) copy-start(s32[9,2,256]{2,1,0:T(2,128)} %a_pnodes.1) | copy-start | bytes 55300
  4.2 0.7 %copy-start.4 = (s32[125,32]{0,1:T(8,128)S(1)}, s32[125,32]{0,1:T(8,128)}, u32[]{:S(2)}) copy-start(s32[125,32]{0,1:T(8,128)} %param.11) | copy-start | bytes 48004
  4.9 0.7 %copy-start.5 = (f32[1280]{0:T(1024)S(1)}, f32[1280]{0:T(1024)}, u32[]{:S(2)}) copy-start(f32[1280]{0:T(1024)} %param.10) | copy-start | bytes 15364

commit v4 on v3

--- a/solution.py
+++ b/solution.py
@@ -424,8 +424,8 @@
             sem, sem, sem, sem, sem, sem, sem, sem,
         ],
         compiler_params=pltpu.CompilerParams(
-            collective_id=0, has_side_effects=True, vmem_limit_bytes=48 * 1024 * 1024
-        ) if REMOTE else pltpu.CompilerParams(has_side_effects=True, vmem_limit_bytes=48 * 1024 * 1024),
+            collective_id=0, has_side_effects=True, vmem_limit_bytes=56 * 1024 * 1024
+        ) if REMOTE else pltpu.CompilerParams(has_side_effects=True, vmem_limit_bytes=56 * 1024 * 1024),
         name="filtered",
     )(*args)
 

time: 61.7 us -> 57.5 us (0.932)
  local copies, waits for them, and re-layouts: 6.22 us -> 1.59 us
    unnamed x19 -> x1, local copies, waits for them, and re-layouts: 6.22 us -> 1.59 us
    pallas_call x1, Pallas kernels: 55 us -> 55.6 us  [shards(): pl.pallas_call(functools.partial(kernel, nx, ny), out_shape=jax.ShapeDtyp...]
where the time goes in v4:
time: 57.5 us; the launch traced here: 57.2 us
  Pallas kernels  55.6 us (97%)
  local copies, waits for them, and re-layouts  1.59 us (3%)
    pallas_call x1, Pallas kernels, shards(): pl.pallas_call(functools.partial(kernel, nx, ny), out_shape=jax.ShapeDtyp...  55.6 us
    unnamed x1, local copies, waits for them, and re-layouts  1.59 us

profile of v4, /device:TPU:1, one launch (start us, length us, event | category | flops | bytes accessed | tf_op | source)
XLA Modules:
  0.0 57.2 jit_solution(16469836742153557952)
XLA Ops:
  0.0 55.6 %filtered.1 = f32[32,1280]{1,0:T(8,128)} custom-call(f32[32,1280]{1,0:T(8,128)} %a_block.1, f32[10,128]{1,0:T(8,128)} %bitcast.5, s32[32,125]{1,0:T(8,128)} %bitcast.4, f32[125,125]{1,0:T(8,128)} %a_stiff.1, s32[8,128]{1,0:T(8,128)} %a_sends.1, s32[9,2,256]{2,1,0:T(2,128)} %a_pnodes.1, f32[9,18,2,256]{3,2,1,0:T(2,128)} %bitcast.3, f32[2,18]{1,0:T(2,128)} %a_coup.1, ...), custom_call_target="tpu_custom_call" | custom-call | tf_op jit(solution)/shard_map/filtered/pallas_call | solution.py:387
  55.6 1.6 %copy.11 = f32[32,1280]{1,0:T(8,128)} copy(f32[32,1280]{1,0:T(8,128)} %filtered.1) | data formatting | bytes 327680

commit v5 on v3

v5 whole, which is shorter than its diff:
```python
import functools

import jax
import jax.numpy as jnp
from jax import lax
from jax.experimental import pallas as pl
from jax.experimental.pallas import tpu as pltpu
from jax.sharding import PartitionSpec as P

DEGREES = 3
CHEB_CENTER = 5.0
CHEB_HALF = 6.0
MESH = pl.DeviceIdType.MESH
OFFS = ((-1, -1), (-1, 0), (-1, 1), (0, -1), (0, 1), (1, -1), (1, 0), (1, 1))
CARD, DIAG = (1, 6, 3, 4), (0, 2, 5, 7)
ORDER = CARD + DIAG
NINE = tuple(k if k < 4 else k + 1 for k in ORDER) + (4,)

VEC = 32
NODE = 1280
OWN = 5
GHO = 4
LO = 256
CN = 125
CELLS = 32
SLOTS = CELLS * 128
SENDS = 1024
PRO = 18
PPAD = 24
PK = 2 * PPAD
PALL = 9 * PK
BF = jnp.bfloat16
F32 = jnp.float32


def split(x):
    hi = x.astype(BF)
    return hi, (x - hi.astype(F32)).astype(BF)


def both(x):
    hi, lo = split(x)
    return jnp.concatenate([hi, lo], axis=0)


def dot(a, b):
    return jnp.dot(a, b, preferred_element_type=F32)


def dot_nt(a, b):
    return lax.dot_general(a, b, (((1,), (1,)), ((), ())), preferred_element_type=F32)


def block_of(got, th):
    row = th * 2 * VEC
    return got[row:row + VEC] + got[row + VEC:row + 2 * VEC]


def picked(got, high, first, count, acc):
    for th in range(count):
        one = block_of(got, th)
        acc = one if acc is None else jnp.where(high == first + th, one, acc)
    return acc


def hot_rows(row, iota):
    return jnp.where(iota == (row & (LO - 1)), 1.0, 0.0).astype(BF)


def kernel(
    nx, ny,
    a_block, a_pot, a_cnodes, a_stiff, a_sends, a_pnodes, a_pvals, a_coup, a_cscale,
    out,
    block, pot, cnodes, stiff, sends, pnodes, pvals, coup, cscale, insem,
    prev, own, cellown, flhs, glhs, klhs, prods, slhs, blhs, eall,
    ct, ohg, hi8, mb, ohs, ohsend, shi8, smb, ohb, same, pn, wf, whi, wlo, twhi, twlo, kf, kmat, crow, cslab,
    sva, rva, svb, rvb, svc, rvc, sve, rve, sem_s, sem_r,
):
    ix = lax.axis_index("mx")
    iy = lax.axis_index("my")

    def at(ox, oy):
        return (lax.rem(ix + ox + nx, nx), lax.rem(iy + oy + ny, ny))

    if REMOTE:
        barrier = pltpu.get_barrier_semaphore()
        for k in ORDER[::-1]:
            pl.semaphore_signal(barrier, inc=1, device_id=at(*OFFS[k]), device_id_type=MESH)

    pairs = (
        (a_sends, sends), (a_block, block), (a_cnodes, cnodes), (a_pnodes, pnodes), (a_pvals, pvals),
        (a_stiff, stiff), (a_coup, coup), (a_cscale, cscale), (a_pot, pot),
    )
    loads = {id(dst): pltpu.make_async_copy(src, dst, insem.at[i]) for i, (src, dst) in enumerate(pairs)}
    for one in loads.values():
        one.start()

    def ready(*refs):
        for ref in refs:
            loads[id(ref)].wait()

    def group(kind, m, first, count):
        src, dst = ((sva, rva), (svb, rvb), (svc, rvc), (sve, rve))[kind]
        sign = (1, -1, 1, -1)[kind]
        sem = 2 * kind + first // 4

        def copy(where, q):
            return pltpu.make_async_remote_copy(
                src_ref=src.at[m, where], dst_ref=dst.at[m, where], send_sem=sem_s.at[sem], recv_sem=sem_r.at[sem],
                device_id=at(sign * OFFS[ORDER[q]][0], sign * OFFS[ORDER[q]][1]), device_id_type=MESH,
            )

        return copy, first, count

    def start(kind, m, first, count):
        if REMOTE:
            copy, first, count = group(kind, m, first, count)
            for q in reversed(range(first, first + count)):
                copy(q, q).start()

    def arrive(kind, m, first, count):
        if REMOTE:
            copy, first, count = group(kind, m, first, count)
            copy(pl.ds(first, count), first).wait_recv()

    def sent(kind, m, first, count):
        if REMOTE:
            copy, first, count = group(kind, m, first, count)
            copy(pl.ds(first, count), first).wait_send()

    def values_at(m, first):
        for j in range(first // 2, first // 2 + 2):
            at_j = slice(j * LO, (j + 1) * LO)
            acc = picked(dot(flhs[...], ohsend[:, at_j]), shi8[0:1, at_j], 0, OWN, None)
            sva[m, 2 * j] = acc[:, 0:128]
            sva[m, 2 * j + 1] = acc[:, 128:256]

    def projector_sums(m, first):
        f2 = both(out[...])
        if first:
            c2 = dot_nt(f2, whi[...])
            c = c2[0:VEC] + c2[VEC:2 * VEC] + dot_nt(f2[0:VEC], wlo[...])
        else:
            c2 = dot(f2, twhi[...])
            c = c2[0:VEC] + c2[VEC:2 * VEC] + dot(f2[0:VEC], twlo[...])
        for q, k in enumerate(NINE):
            piece = c[:, k * PK:(k + 1) * PK]
            if q == 8:
                cslab[:, 0:PK] = piece[0:16]
                cslab[:, 64:64 + PK] = piece[16:32]
            else:
                svc[m, q, :, 0:PK] = piece[0:16]
                svc[m, q, :, 64:64 + PK] = piece[16:32]
        start(2, m, 0, 8)

    def field_rows(field):
        for th in range(OWN):
            flhs[th * 2 * VEC:(th + 1) * 2 * VEC, :] = both(field[:, th * LO:(th + 1) * LO])

    sub = lax.broadcasted_iota(jnp.int32, (LO, 128), 0)
    ready(sends)
    for q, k in enumerate(ORDER):
        at_q = slice(q * 128, (q + 1) * 128)
        row = sends[k:k + 1, :]
        ohsend[:, at_q] = hot_rows(row, sub)
        shi8[:, at_q] = jnp.broadcast_to(row >> 8, (8, 128))
    ready(block)
    out[...] = block[...]
    field_rows(out)

    values_at(0, 4)
    if REMOTE:
        pl.semaphore_wait(barrier, 8)
    start(0, 0, 4, 4)
    values_at(0, 0)
    start(0, 0, 0, 4)

    ready(pnodes, pvals)
    pn[...] = jnp.zeros_like(pn)
    for k in range(9):
        pn[2 * k:2 * k + 2, :] = pnodes[k]
    pcols = jnp.concatenate([pn[:, 0:128].T, pn[:, 128:256].T], axis=0)
    lane2 = lax.broadcasted_iota(jnp.int32, (LO, LO), 1)
    pad = jnp.zeros((PPAD - PRO, LO), F32)
    for k in range(9):
        parts = []
        for a in range(2):
            row = pnodes[k, a:a + 1, :]
            high = jnp.broadcast_to(row >> 8, (16, LO))
            v = jnp.concatenate([pvals[k, :, a, :], pad], axis=0)
            vhi = v.astype(BF).astype(F32)
            v2 = jnp.concatenate([vhi, v - vhi], axis=0).astype(BF)
            rows = []
            for th in range(OWN):
                mask = jnp.where(high == th, 1.0, 0.0).astype(BF)
                rows.append(v2 * jnp.concatenate([mask] * 3, axis=0))
            col = jnp.broadcast_to(pcols[:, 2 * k + a:2 * k + a + 1], (LO, LO))
            got = dot(jnp.concatenate(rows, axis=0), hot_rows(col, lane2))
            parts.append([got[th * PK:th * PK + PPAD] + got[th * PK + PPAD:(th + 1) * PK] for th in range(OWN)])
        for th in range(OWN):
            at_t = slice(th * LO, (th + 1) * LO)
            w = jnp.concatenate([parts[0][th], parts[1][th]], axis=0)
            hi, lo = split(w)
            wf[k * PK:(k + 1) * PK, at_t] = w
            whi[k * PK:(k + 1) * PK, at_t] = hi
            wlo[k * PK:(k + 1) * PK, at_t] = lo
    for m in range(DEGREES):
        for k in range(8):
            svc[m, k] = jnp.zeros((16, 128), F32)
    cslab[...] = jnp.zeros_like(cslab)
    projector_sums(0, True)

    ct[...] = jnp.full((128, 128), -1, jnp.int32)
    ready(cnodes)
    ct[0:CELLS, 0:CN] = cnodes[...]
    pos = ct[0:CELLS, :]
    slot = (pos >> 7) - 2 * OWN
    new = slot
    for q, k in enumerate(ORDER):
        new = jnp.where(slot == k, q, new)
    ct[0:CELLS, :] = jnp.where(slot >= 0, ((new + 2 * OWN) << 7) + (pos & 127), pos)
    for q, k in enumerate(ORDER):
        ct[CELLS + q:CELLS + q + 1, :] = sends[k:k + 1, :]
    cols = ct[...].T
    lane = lax.broadcasted_iota(jnp.int32, (128, LO), 1)
    for c in range(CELLS):
        at_c = slice(c * 128, (c + 1) * 128)
        row = ct[c:c + 1, :]
        ohg[:, at_c] = hot_rows(row, sub)
        ohs[at_c, :] = hot_rows(jnp.broadcast_to(cols[:, c:c + 1], (128, LO)), lane)
        high = jnp.broadcast_to(row >> 8, (16, 128))
        hi8[:, at_c] = high[0:8]
        for th in range(OWN + GHO):
            mb[th, :, at_c] = jnp.where(high == th, 1.0, 0.0).astype(BF)
    for q in range(8):
        at_q = slice(q * 128, (q + 1) * 128)
        high = jnp.broadcast_to(ct[CELLS + q:CELLS + q + 1, :] >> 8, (16, 128))
        ohb[at_q, :] = hot_rows(jnp.broadcast_to(cols[:, CELLS + q:CELLS + q + 1], (128, LO)), lane)
        for th in range(OWN):
            smb[th, :, at_q] = jnp.where(high == th, 1.0, 0.0).astype(BF)
    for q in range(4):
        col = jnp.broadcast_to(cols[:, CELLS + 4 + q:CELLS + 5 + q], (128, 128))
        for p in range(4):
            hit = col == ct[CELLS + 4 + p:CELLS + 5 + p, :]
            same[q * 128:(q + 1) * 128, p * 128:(p + 1) * 128] = jnp.where(hit, 1.0, 0.0).astype(BF)

    ready(stiff, coup, cscale, pot)
    kf[...] = jnp.zeros((128, 128), F32)
    kf[0:CN, 0:CN] = stiff[...]
    khi, klo = split(kf[...])
    for r in range(2):
        kmat[r * 128:(r + 1) * 128, 0:128] = khi
        kmat[r * 128:(r + 1) * 128, 128:256] = klo

    crow[...] = jnp.zeros_like(crow)
    for h in range(2):
        for a in range(2):
            first = 64 * h + PPAD * a
            crow[0:1, first:first + PRO] = coup[a:a + 1, :]
    prev[...] = jnp.zeros_like(prev)


    def turned():
        wf[PALL:512, :] = jnp.zeros((512 - PALL, NODE), F32)
        for n in range(NODE // 128):
            at_n = slice(n * 128, (n + 1) * 128)
            for r in range(4):
                at_r = slice(r * 128, (r + 1) * 128)
                hi, lo = split(wf[at_r, at_n].T)
                twhi[at_n, at_r] = hi
                twlo[at_n, at_r] = lo

    def masked_rows(pair, first, count, at_c):
        for th in range(first, first + count):
            slhs[th * 2 * VEC:(th + 1) * 2 * VEC, at_c] = pair * jnp.concatenate([mb[th, :, at_c]] * 4, axis=0)

    def scatter_rows(first, count):
        for c in range(SLOTS // 512):
            at_c = slice(c * 512, (c + 1) * 512)
            masked_rows(prods[:, at_c], first, count, at_c)
        return dot(slhs[first * 2 * VEC:(first + count) * 2 * VEC, :], ohs[...])

    ghosts_in = rva if REMOTE else sva
    replies_in = rvb if REMOTE else svb
    sums_in = rvc if REMOTE else svc
    coefs_in = rve if REMOTE else sve

    def apply(m, carry):
        for j in range(SLOTS // LO):
            at_j = slice(j * LO, (j + 1) * LO)
            acc = picked(dot(flhs[...], ohg[:, at_j]), hi8[0:1, at_j], 0, OWN, None)
            cellown[:, at_j] = jnp.where(hi8[0:1, at_j] >= 0, acc, 0.0)

        def ghost_rows(first):
            arrive(0, m, 2 * first, 4)
            for t in range(first, first + 2):
                glhs[t * 2 * VEC:(t + 1) * 2 * VEC, 0:128] = both(ghosts_in[m, 2 * t])
                glhs[t * 2 * VEC:(t + 1) * 2 * VEC, 128:256] = both(ghosts_in[m, 2 * t + 1])

        def ghost_columns(first, at_j):
            got = dot(glhs[first * 2 * VEC:(first + 2) * 2 * VEC, :], ohg[:, at_j])
            return picked(got, hi8[0:1, at_j], OWN + first, 2, cellown[:, at_j])

        ghost_rows(0)
        for j in range(SLOTS // LO):
            at_j = slice(j * LO, (j + 1) * LO)
            cellown[:, at_j] = ghost_columns(0, at_j)
        sent(0, m, 0, 4)
        sent(2, m, 0, 8)

        ghost_rows(2)
        got = None
        for g in range(4):
            for j in range(4 * g, 4 * g + 4):
                hi, lo = split(ghost_columns(2, slice(j * LO, (j + 1) * LO)))
                for h in range(2):
                    rows = slice((2 * j + h) * VEC, (2 * j + h + 1) * VEC)
                    klhs[rows, 0:128] = hi[:, h * 128:(h + 1) * 128]
                    klhs[rows, 128:256] = lo[:, h * 128:(h + 1) * 128]
            prod2 = dot(klhs[g * 256:(g + 1) * 256, :], kmat[...])
            prod = prod2[:, 0:128] + prod2[:, 128:256]
            for i in range(8):
                c0 = g * 8 + i
                at_c = slice(c0 * 128, (c0 + 1) * 128)
                pair = both(prod[i * VEC:(i + 1) * VEC] * cscale[c0])
                prods[:, at_c] = pair
                masked_rows(pair, OWN + 2, 2, at_c)
            at_g = slice(g * 1024, (g + 1) * 1024)
            some = dot(slhs[(OWN + 2) * 2 * VEC:(OWN + 4) * 2 * VEC, at_g], ohs[at_g, :])
            got = some if got is None else got + some
            if g == 2:
                arrive(2, m, 0, 8)
                total = cslab[...]
                for q in range(8):
                    total = total + sums_in[m, q]
                coef = total * crow[0:1, :]
                for q in range(8):
                    sve[m, q] = coef
                start(3, m, 0, 8)

        def give_back(first, got):
            for t in range(2):
                one = block_of(got, t)
                svb[m, 2 * (first + t)] = one[:, 0:128]
                svb[m, 2 * (first + t) + 1] = one[:, 128:256]
            start(1, m, 2 * first, 4)

        give_back(2, got)
        give_back(0, scatter_rows(OWN, 2))

        got = scatter_rows(0, OWN)
        for n in range(NODE // 128):
            at_n = slice(n * 128, (n + 1) * 128)
            own[:, at_n] = (pot[n:n + 1, :] - CHEB_CENTER) * out[:, at_n]
        for th in range(OWN):
            own[:, th * LO:(th + 1) * LO] += block_of(got, th)
        sent(0, m, 4, 4)

        @pl.when(m == 0)
        def _():
            turned()

        arrive(3, m, 0, 8)
        for q, k in enumerate(NINE):
            slab = coef if q == 8 else coefs_in[m, q]
            eall[0:16, k * PK:(k + 1) * PK] = slab[:, 0:PK]
            eall[16:32, k * PK:(k + 1) * PK] = slab[:, 64:64 + PK]
        e2 = both(eall[...])
        s2 = dot(e2, whi[...])
        own[...] += s2[0:VEC] + s2[VEC:2 * VEC] + dot(e2[0:VEC], wlo[...])

        def reply_rows(first):
            for q in range(first, first + 4):
                at_q = slice(q * 128, (q + 1) * 128)
                pair = both(replies_in[m, q])
                for th in range(OWN):
                    blhs[th * 2 * VEC:(th + 1) * 2 * VEC, at_q] = pair * jnp.concatenate([smb[th, :, at_q]] * 4, axis=0)
            at_f = slice(first * 128, (first + 4) * 128)
            return dot(blhs[:, at_f], ohb[at_f, :])

        alpha = jnp.where(m == 0, 1.0 / CHEB_HALF, 2.0 / CHEB_HALF)
        arrive(1, m, 0, 4)
        got = reply_rows(0)
        for th in range(OWN):
            at_t = slice(th * LO, (th + 1) * LO)
            own[:, at_t] = alpha * (own[:, at_t] + block_of(got, th)) - prev[:, at_t]

        @pl.when(m < DEGREES - 1)
        def _():
            field_rows(own)
            values_at(m + 1, 4)

        arrive(1, m, 4, 4)

        @pl.when(m < DEGREES - 1)
        def _():
            pair = jnp.concatenate([both(replies_in[m, q]) for q in range(4, 8)], axis=1)
            got = dot(pair, same[...])
            more = alpha * (got[0:VEC] + got[VEC:2 * VEC])
            for q in range(4):
                sva[m + 1, 4 + q] += more[:, q * 128:(q + 1) * 128]
            start(0, m + 1, 4, 4)

        got = reply_rows(4)
        for th in range(OWN):
            at_t = slice(th * LO, (th + 1) * LO)
            new = own[:, at_t] + alpha * block_of(got, th)
            prev[:, at_t] = out[:, at_t]
            out[:, at_t] = new

        @pl.when(m < DEGREES - 1)
        def _():
            field_rows(out)
            values_at(m + 1, 0)
            start(0, m + 1, 0, 4)
            projector_sums(m + 1, False)

        sent(1, m, 0, 4)
        sent(1, m, 4, 4)
        sent(3, m, 0, 8)
        return carry

    lax.fori_loop(0, DEGREES, apply, 0)


REMOTE = True


def shards(block, potential, cell_nodes, cell_scale, stiffness, send_nodes, proj_nodes, proj_values, coupling):
    nx, ny = lax.axis_size("mx"), lax.axis_size("my")
    vmem = pl.BlockSpec(memory_space=pltpu.VMEM)
    halo = pltpu.VMEM((DEGREES, 8, VEC, 128), F32)
    slab = pltpu.VMEM((DEGREES, 8, 16, 128), F32)
    sem = pltpu.SemaphoreType.DMA((8,))
    hbm = pl.BlockSpec(memory_space=pltpu.HBM)
    args = (
        block, potential.reshape(NODE // 128, 128), cell_nodes.T, stiffness, send_nodes, proj_nodes,
        proj_values.transpose(0, 2, 1, 3), coupling, cell_scale,
    )
    args = tuple(pltpu.with_memory_space_constraint(one, pltpu.HBM) for one in args)
    return pl.pallas_call(
        functools.partial(kernel, nx, ny),
        out_shape=jax.ShapeDtypeStruct((VEC, NODE), F32),
        in_specs=[hbm] * len(args),
        out_specs=vmem,
        scratch_shapes=[pltpu.VMEM(one.shape, one.dtype) for one in args[:-1]] + [
            pltpu.SMEM(cell_scale.shape, F32),
            pltpu.SemaphoreType.DMA((len(args),)),
            pltpu.VMEM((VEC, NODE), F32),
            pltpu.VMEM((VEC, NODE), F32),
            pltpu.VMEM((VEC, SLOTS), F32),
            pltpu.VMEM((OWN * 2 * VEC, LO), BF),
            pltpu.VMEM((GHO * 2 * VEC, LO), BF),
            pltpu.VMEM((CELLS * VEC, 256), BF),
            pltpu.VMEM((2 * VEC, SLOTS), BF),
            pltpu.VMEM(((OWN + GHO) * 2 * VEC, SLOTS), BF),
            pltpu.VMEM((OWN * 2 * VEC, SENDS), BF),
            pltpu.VMEM((VEC, PALL), F32),
            pltpu.VMEM((128, 128), jnp.int32),
            pltpu.VMEM((LO, SLOTS), BF),
            pltpu.VMEM((8, SLOTS), jnp.int32),
            pltpu.VMEM((OWN + GHO, 16, SLOTS), BF),
            pltpu.VMEM((SLOTS, LO), BF),
            pltpu.VMEM((LO, SENDS), BF),
            pltpu.VMEM((8, SENDS), jnp.int32),
            pltpu.VMEM((OWN, 16, SENDS), BF),
            pltpu.VMEM((SENDS, LO), BF),
            pltpu.VMEM((512, 512), BF),
            pltpu.VMEM((128, LO), jnp.int32),
            pltpu.VMEM((512, NODE), F32),
            pltpu.VMEM((PALL, NODE), BF),
            pltpu.VMEM((PALL, NODE), BF),
            pltpu.VMEM((NODE, 512), BF),
            pltpu.VMEM((NODE, 512), BF),
            pltpu.VMEM((128, 128), F32),
            pltpu.VMEM((256, 256), BF),
            pltpu.VMEM((8, 128), F32),
            pltpu.VMEM((16, 128), F32),
            halo, halo, halo, halo, slab, slab, slab, slab,
            sem, sem,
        ],
        compiler_params=pltpu.CompilerParams(
            collective_id=0, has_side_effects=True, vmem_limit_bytes=48 * 1024 * 1024
        ) if REMOTE else pltpu.CompilerParams(has_side_effects=True, vmem_limit_bytes=48 * 1024 * 1024),
        name="filtered",
    )(*args)


def solution(mesh):
    axes = ("mx", "my")
    placed = (
        P(None, axes), P(axes), P(None, axes), P(axes), P(), P(None, axes),
        P(None, axes, None), P(None, axes, None, None), P(axes, None),
    )
    return jax.shard_map(shards, mesh=mesh, in_specs=placed, out_specs=P(None, axes), check_vma=False)
```

time: 61.7 us -> 53.6 us (0.87)
  local copies, waits for them, and re-layouts: 6.22 us -> 0.67 us
  Pallas kernels: 55 us -> 52.8 us
    unnamed x19 -> x1, local copies, waits for them, and re-layouts: 6.22 us -> 0.67 us
    pallas_call x1, Pallas kernels: 55 us -> 52.8 us  [shards(): pl.pallas_call(functools.partial(kernel, nx, ny), out_shape=jax.ShapeDtyp...]
where the time goes in v5:
time: 53.6 us; the launch traced here: 53.5 us
  Pallas kernels  52.8 us (99%)
  local copies, waits for them, and re-layouts  0.67 us (1%)
    pallas_call x1, Pallas kernels, shards(): pl.pallas_call(functools.partial(kernel, nx, ny), out_shape=jax.ShapeDtyp...  52.8 us

profile of v5, /device:TPU:1, one launch (start us, length us, event | category | flops | bytes accessed | tf_op | source)
XLA Modules:
  0.0 53.5 jit_solution(7577966553893092513)
XLA Ops:
  0.0 52.8 %filtered.1 = f32[32,1280]{1,0:T(8,128)S(1)} custom-call(f32[32,1280]{1,0:T(8,128)} %a_block.1, f32[10,128]{1,0:T(8,128)} %bitcast.5, s32[32,125]{1,0:T(8,128)} %bitcast.4, f32[125,125]{1,0:T(8,128)} %a_stiff.1, s32[8,128]{1,0:T(8,128)} %a_sends.1, s32[9,2,256]{2,1,0:T(2,128)} %a_pnodes.1, f32[9,18,2,256]{3,2,1,0:T(2,128)} %bitcast.3, f32[2,18]{1,0:T(2,128)} %a_coup.1, ...), custom_call_target="tpu_custom_call" | custom-call | tf_op jit(solution)/shard_map/filtered/pallas_call | solution.py:441
  52.8 0.7 %copy.11 = f32[32,1280]{1,0:T(8,128)} copy(f32[32,1280]{1,0:T(8,128)S(1)} %filtered.1) | data formatting | bytes 327680

commit v6 on v5

--- a/solution.py
+++ b/solution.py
@@ -169,11 +169,7 @@
     field_rows(out)
 
     values_at(0, 4)
-    if REMOTE:
-        pl.semaphore_wait(barrier, 8)
-    start(0, 0, 4, 4)
     values_at(0, 0)
-    start(0, 0, 0, 4)
 
     ready(pnodes, pvals)
     pn[...] = jnp.zeros_like(pn)
@@ -208,6 +204,10 @@
         for k in range(8):
             svc[m, k] = jnp.zeros((16, 128), F32)
     cslab[...] = jnp.zeros_like(cslab)
+    if REMOTE:
+        pl.semaphore_wait(barrier, 8)
+    start(0, 0, 4, 4)
+    start(0, 0, 0, 4)
     projector_sums(0, True)
 
     ct[...] = jnp.full((128, 128), -1, jnp.int32)

time: 53.6 us -> 52.3 us (0.976)
  Pallas kernels: 52.8 us -> 51.5 us
    pallas_call x1, Pallas kernels: 52.8 us -> 51.5 us  [shards(): pl.pallas_call(functools.partial(kernel, nx, ny), out_shape=jax.ShapeDtyp...]
where the time goes in v6:
time: 52.3 us; the launch traced here: 52.1 us
  Pallas kernels  51.5 us (98%)
  local copies, waits for them, and re-layouts  0.67 us (1%)
    pallas_call x1, Pallas kernels, shards(): pl.pallas_call(functools.partial(kernel, nx, ny), out_shape=jax.ShapeDtyp...  51.5 us

profile of v6, /device:TPU:1, one launch (start us, length us, event | category | flops | bytes accessed | tf_op | source)
XLA Modules:
  0.0 52.1 jit_solution(8899807376343789239)
XLA Ops:
  0.0 51.5 %filtered.1 = f32[32,1280]{1,0:T(8,128)S(1)} custom-call(f32[32,1280]{1,0:T(8,128)} %a_block.1, f32[10,128]{1,0:T(8,128)} %bitcast.5, s32[32,125]{1,0:T(8,128)} %bitcast.4, f32[125,125]{1,0:T(8,128)} %a_stiff.1, s32[8,128]{1,0:T(8,128)} %a_sends.1, s32[9,2,256]{2,1,0:T(2,128)} %a_pnodes.1, f32[9,18,2,256]{3,2,1,0:T(2,128)} %bitcast.3, f32[2,18]{1,0:T(2,128)} %a_coup.1, ...), custom_call_target="tpu_custom_call" | custom-call | tf_op jit(solution)/shard_map/filtered/pallas_call | solution.py:441
  51.5 0.7 %copy.11 = f32[32,1280]{1,0:T(8,128)} copy(f32[32,1280]{1,0:T(8,128)S(1)} %filtered.1) | data formatting | bytes 327680

commit v7 on v6

--- a/solution.py
+++ b/solution.py
@@ -151,7 +151,8 @@
             else:
                 svc[m, q, :, 0:PK] = piece[0:16]
                 svc[m, q, :, 64:64 + PK] = piece[16:32]
-        start(2, m, 0, 8)
+        if not first:
+            start(2, m, 0, 8)
 
     def field_rows(field):
         for th in range(OWN):
@@ -204,11 +205,12 @@
         for k in range(8):
             svc[m, k] = jnp.zeros((16, 128), F32)
     cslab[...] = jnp.zeros_like(cslab)
+    projector_sums(0, True)
     if REMOTE:
         pl.semaphore_wait(barrier, 8)
     start(0, 0, 4, 4)
     start(0, 0, 0, 4)
-    projector_sums(0, True)
+    start(2, 0, 0, 8)
 
     ct[...] = jnp.full((128, 128), -1, jnp.int32)
     ready(cnodes)

time: 52.3 us -> 52.1 us (level)
  no operation moved by 1% of the time
where the time goes in v7:
time: 52.1 us; the launch traced here: 52 us
  Pallas kernels  51.3 us (98%)
  local copies, waits for them, and re-layouts  0.67 us (1%)
    pallas_call x1, Pallas kernels, shards(): pl.pallas_call(functools.partial(kernel, nx, ny), out_shape=jax.ShapeDtyp...  51.3 us

profile of v7, /device:TPU:1, one launch (start us, length us, event | category | flops | bytes accessed | tf_op | source)
XLA Modules:
  0.0 52.0 jit_solution(9773699044680962361)
XLA Ops:
  0.0 51.3 %filtered.1 = f32[32,1280]{1,0:T(8,128)S(1)} custom-call(f32[32,1280]{1,0:T(8,128)} %a_block.1, f32[10,128]{1,0:T(8,128)} %bitcast.5, s32[32,125]{1,0:T(8,128)} %bitcast.4, f32[125,125]{1,0:T(8,128)} %a_stiff.1, s32[8,128]{1,0:T(8,128)} %a_sends.1, s32[9,2,256]{2,1,0:T(2,128)} %a_pnodes.1, f32[9,18,2,256]{3,2,1,0:T(2,128)} %bitcast.3, f32[2,18]{1,0:T(2,128)} %a_coup.1, ...), custom_call_target="tpu_custom_call" | custom-call | tf_op jit(solution)/shard_map/filtered/pallas_call | solution.py:443
  51.3 0.7 %copy.11 = f32[32,1280]{1,0:T(8,128)} copy(f32[32,1280]{1,0:T(8,128)S(1)} %filtered.1) | data formatting | bytes 327680
